TPU v7x, 256 devices: a whole 4x4x8 slice. The times are simulated.
256 devices in a mesh: bins: 128 (over z, x_hi, y, core), diag: 2 (over x_lo).
Axes of the slice: x: 4 (x_hi: 2, x_lo: 2; x = x_hi * 2 + x_lo), y: 4, z: 8, core: 2. Of those that a mesh axis runs over, the one named last changes fastest.
Arguments:
- features: bfloat16 [32, 192, 16384], P(None, 'diag', 'bins'), may hold values from -6 to 6
- cotangent: bfloat16 [32, 192, 16384], P(None, 'diag', 'bins'), may hold values from -6 to 6
- band_mask: int32 [192, 16384], P('diag', 'bins'), may hold values 0 or 1
- dilation: int32 [2], replicated, may hold values from 1 to 8, as said below
- w_first: bfloat16 [32, 9, 32], replicated, may hold values from -0.375 to 0.375
- b_first: float32 [32], replicated, may hold values from -3 to 3
- w_second: bfloat16 [32, 9, 32], replicated, may hold values from -0.375 to 0.375
Outputs:
- output: bfloat16 [32, 192, 16384], P(None, 'diag', 'bins')
- grad_features: bfloat16 [32, 192, 16384], P(None, 'diag', 'bins')
- grad_w_first: float32 [32, 9, 32], replicated
- grad_b_first: float32 [32], replicated
- grad_w_second: float32 [32, 9, 32], replicated
Inputs may be any that keep to these rules, and one draw needn't show every extreme that they name: Entry k is the dilation rate of convolution k; one of the two equals 8.
All inputs are finite; a program needn't handle non-finite values. No bound on the sum of `band_mask` on one device may be relied on, other than what follows from the above.
Results may differ from a plain program's by a relative error of at most 0.013.
Values may be sent and summed in bfloat16 or wider, within the bound.
A program may use at most 128 MiB of HBM per device.

v0:
```python
import jax
import jax.numpy as jnp
from jax import lax
from jax.sharding import PartitionSpec as P

OFF = 192
RMAX = 8


def with_halo(shard, sides, width):
    for axis, dim in sides:
        size, length = (lax.axis_size(axis), shard.shape[dim])
        up = [(i, (i + 1) % size) for i in range(size - 1)]
        down = [(j, i) for i, j in up]
        last = lax.slice_in_dim(shard, length - width, length, axis=dim)
        initial = lax.slice_in_dim(shard, 0, width, axis=dim)
        before = lax.ppermute(last, axis, up)
        after = lax.ppermute(initial, axis, down)
        shard = jnp.concatenate([before, shard, after], axis=dim)
    return shard


def dsilu(values):
    squash = jax.nn.sigmoid(values)
    return squash * (1.0 + values * (1.0 - squash))


def extend(field_in):
    wider = with_halo(field_in, (("diag", 1),), 2 * RMAX)
    return with_halo(wider, (("bins", 2),), RMAX)


def local_patches(padded, rate_value, flip_sign, offsets, columns):
    pieces = []
    for a_off in (-1, 0, 1):
        for b_off in (-1, 0, 1):
            d_start = 2 * RMAX + flip_sign * (b_off - a_off) * rate_value
            i_start = RMAX + flip_sign * a_off * rate_value
            pieces.append(
                lax.dynamic_slice(
                    padded, (jnp.int32(0), d_start, i_start), (padded.shape[0], offsets, columns)
                )
            )
    return jnp.concatenate(pieces, axis=0)


def apply_taps(matrix, patches):
    return jnp.einsum("ok,kdi->odi", matrix, patches, preferred_element_type=jnp.float32)


def tap_sums(upstream, patches):
    return jnp.einsum("odi,kdi->ok", upstream, patches, preferred_element_type=jnp.float32)


def shards(features, cotangent, band_mask, dilation, w_first, b_first, w_second):
    channels, offsets, columns = features.shape
    mask_float = band_mask.astype(jnp.float32)[None]
    rate_one = dilation[0]
    rate_two = dilation[1]
    matrix_one = w_first.reshape(channels, 9 * channels)
    matrix_two = w_second.reshape(channels, 9 * channels)
    trans_one = jnp.transpose(w_first, (2, 1, 0)).reshape(channels, 9 * channels)
    trans_two = jnp.transpose(w_second, (2, 1, 0)).reshape(channels, 9 * channels)
    factor = 1.0 / jnp.sqrt(jnp.float32(OFF) * jnp.float32(columns * lax.axis_size("bins")))
    feat_full = features.astype(jnp.float32)
    upstream = cotangent.astype(jnp.float32)
    act_in = (jax.nn.silu(feat_full) * mask_float).astype(jnp.bfloat16)
    patches_one = local_patches(extend(act_in), rate_one, 1, offsets, columns)
    pre_act = apply_taps(matrix_one, patches_one) + b_first[:, None, None]
    hidden = (jax.nn.silu(pre_act) * mask_float).astype(jnp.bfloat16)
    patches_two = local_patches(extend(hidden), rate_two, 1, offsets, columns)
    output = (feat_full + mask_float * apply_taps(matrix_two, patches_two)).astype(jnp.bfloat16)
    grad_out = (upstream * mask_float).astype(jnp.bfloat16)
    local_two = tap_sums(grad_out, patches_two)
    grad_hid = apply_taps(
        trans_two, local_patches(extend(grad_out), rate_two, -1, offsets, columns)
    )
    grad_pre = (grad_hid * mask_float * dsilu(pre_act)).astype(jnp.bfloat16)
    grad_act = apply_taps(
        trans_one, local_patches(extend(grad_pre), rate_one, -1, offsets, columns)
    )
    local_one = tap_sums(grad_pre, patches_one)
    local_bias = jnp.sum(grad_pre.astype(jnp.float32), axis=(1, 2))
    grad_features = (upstream + mask_float * dsilu(feat_full) * grad_act).astype(jnp.bfloat16)
    total_one, total_bias, total_two = lax.psum(
        (local_one, local_bias, local_two), ("bins", "diag")
    )
    grad_one = (total_one * factor).reshape(channels, 9, channels)
    grad_two = (total_two * factor).reshape(channels, 9, channels)
    return (output, grad_features, grad_one, total_bias * factor, grad_two)


def solution(mesh):
    in_specs = (
        P(None, "diag", "bins"),
        P(None, "diag", "bins"),
        P("diag", "bins"),
        P(),
        P(),
        P(),
        P(),
    )
    out_specs = (P(None, "diag", "bins"), P(None, "diag", "bins"), P(), P(), P())
    return jax.shard_map(shards, mesh=mesh, in_specs=in_specs, out_specs=out_specs, check_vma=False)
```

profile of v0, /device:TPU:1, one launch (start us, length us, event | category | flops | bytes accessed | tf_op | source)
XLA Modules:
  0.0 427.0 jit_solution(10116279884496655369)
XLA Ops:
  9.7 4.0 collective-permute-start
  15.8 3.7 collective-permute-done.1
  20.0 1.7 copy.35
  21.7 5.2 %collective-permute-start.2 = (bf16[32,128,8]{1,2,0:T(8,128)(2,1)}, bf16[32,128,8]{1,2,0:T(8,128)(2,1)S(1)}, u32[]{:S(2)}, u32[]{:S(2)}) collective-permute-start(bf16[32,128,8]{1,2,0:T(8,128)(2,1)} %copy.35), channel_id=1, source_target_pairs={{0,2},{2,4},{4,6},{6,8},{8,10},{10,12},{12,14},{14,16},{16,18},{18... | collective-permute-start | bytes 196616 | tf_op jit(solution)/shard_map/ppermute | solution.py:17
  28.0 2.1 collective-permute-start.3
  41.6 2.3 copy.38
  43.9 1.9 pad_maximum_fusion
  50.0 3.3 fusion
  56.6 4.0 collective-permute-start.8
  64.2 4.6 %collective-permute-start.6 = (bf16[32,128,8]{1,2,0:T(8,128)(2,1)}, bf16[32,128,8]{1,2,0:T(8,128)(2,1)}, u32[]{:S(2)}, u32[]{:S(2)}) collective-permute-start(bf16[32,128,8]{1,2,0:T(8,128)(2,1)} %copy.41), channel_id=1, source_target_pairs={{0,2},{2,4},{4,6},{6,8},{8,10},{10,12},{12,14},{14,16},{16,18},{18... | collective-permute-start | bytes 196616 | tf_op jit(solution)/shard_map/ppermute | solution.py:17
  70.5 1.9 collective-permute-start.7
  74.6 3.6 collective-permute-start.10
  80.0 1.9 collective-permute-start.11
  81.9 3.2 copy.43
  85.1 3.2 copy.44
  88.3 3.2 pad_maximum_fusion.1
  94.1 3.1 copy.50
  97.2 3.2 copy.51
  100.4 3.5 pad_maximum_fusion.2
  107.2 1.7 dynamic-slice_dynamic-update-slice_fusion.8
  108.9 2.4 convert_reduce_fusion
  111.3 2.7 convolution_bitcast_fusion.1
  121.5 5.8 %convolution_bitcast_fusion = f32[32,288]{1,0:T(8,128)} fusion(bf16[32,96,128]{2,0,1:T(8,128)(2,1)S(1)} %get-tuple-element.39, bf16[288,96,128]{2,0,1:T(8,128)(2,1)} %dynamic-slice_dynamic-update-slice_fusion.16), kind=kOutput, calls=%fused_computation.36 | convolution fusion | flops 226492416 | bytes 7901184 | tf_op jit(solution)/shard_map/odi,kdi->ok/dot_general | solution.py:52
  127.3 4.3 collective-permute-start.12
  132.9 4.6 %fusion.7 = bf16[32,96,128]{2,0,1:T(8,128)(2,1)S(1)} fusion(bf16[288,96,128]{2,0,1:T(8,128)(2,1)} %dynamic-slice_dynamic-update-slice_fusion.16, bf16[32,288,1]{0,1,2:T(8,128)(2,1)S(1)} %bitcast.94, f32[96,128]{1,0:T(8,128)S(1)} %convert_element_type.31, bf16[32,96,128]{2,1,0:T(8,128)(2,1)S(1)} %copy-done.6), kind=kOutput, calls=%fused_computation.17 | convolution fusion | flops 228065280 | bytes 8718336 | tf_op jit(solution)/shard_map/ok,kdi->odi/dot_general | solution.py:48
  138.7 253.5 %all-reduce.3.cloned.1.call-done = (f32[32,288]{1,0:T(8,128)}, f32[32]{0:T(128)}, f32[32,288]{1,0:T(8,128)}) async-done(((f32[32,288]{1,0:T(8,128)}, f32[32]{0:T(128)}, f32[32,288]{1,0:T(8,128)}), (f32[32,288]{1,0:T(8,128)}, f32[32]{0:T(128)}, f32[32,288]{1,0:T(8,128)})) %all-reduce.3.cloned.1.call-update) | async-done | bytes 73872 | tf_op jit(solution)/shard_map/psum | solution.py:85
  395.3 2.2 copy.53
  397.5 3.4 collective-permute-start.14
  402.0 1.9 collective-permute-start.15
  407.6 2.3 copy.56
  410.0 2.9 pad_maximum_fusion.3
  416.6 2.1 fusion.1
  (129 shorter events, 53.5 us)
Async XLA Ops:
  7.2 385.0 %all-reduce.3.cloned.1.call-start = ((), (), s32[]{:S(2)}) async-start(), calls=%async_computation | async-start | bytes 197632 | tf_op jit(solution)/shard_map/psum | solution.py:85
  9.7 6.1 %collective-permute-start = (bf16[32,16,128]{2,0,1:T(8,128)(2,1)S(1)}, bf16[32,16,128]{2,0,1:T(8,128)(2,1)S(1)}, u32[]{:S(2)}, u32[]{:S(2)}) collective-permute-start(bf16[32,16,128]{2,0,1:T(8,128)(2,1)S(1)} %get-tuple-element.37), channel_id=1, source_target_pairs={{0,1},{2,3},{4,5},{6,7},{8,9},{10,11},{12,13},{14,15},{16,17},{18,... | collective-permute-start | bytes 393224 | tf_op jit(solution)/shard_map/ppermute | solution.py:17
  13.6 16.4 %copy-start.11 = (s32[2]{0:T(128)S(1)}, s32[2]{0:T(128)}, u32[]{:S(2)}) copy-start(s32[2]{0:T(128)} %param.10) | copy-start | bytes 28
  13.7 26.1 %copy-start.9 = (bf16[32,9,32]{2,0,1:T(8,128)(2,1)S(1)}, bf16[32,9,32]{2,0,1:T(8,128)(2,1)}, u32[]{:S(2)}) copy-start(bf16[32,9,32]{2,0,1:T(8,128)(2,1)} %param.11) | copy-start | bytes 55300
  13.7 26.3 %copy-start.7 = (bf16[32,9,32]{2,0,1:T(8,128)(2,1)S(1)}, bf16[32,9,32]{2,0,1:T(8,128)(2,1)}, u32[]{:S(2)}) copy-start(bf16[32,9,32]{2,0,1:T(8,128)(2,1)} %param.13) | copy-start | bytes 55300
  13.7 5.8 %collective-permute-start.1 = (bf16[32,16,128]{2,0,1:T(8,128)(2,1)S(1)}, bf16[32,16,128]{2,0,1:T(8,128)(2,1)S(1)}, u32[]{:S(2)}, u32[]{:S(2)}) collective-permute-start(bf16[32,16,128]{2,0,1:T(8,128)(2,1)S(1)} %get-tuple-element.38), channel_id=1, source_target_pairs={{1,0},{3,2},{5,4},{7,6},{9,8},{11,10},{13,12},{15,14},{17,16},{19,... | collective-permute-start | bytes 393224 | tf_op jit(solution)/shard_map/ppermute | solution.py:18
  21.7 18.4 %collective-permute-start.2 = (bf16[32,128,8]{1,2,0:T(8,128)(2,1)}, bf16[32,128,8]{1,2,0:T(8,128)(2,1)S(1)}, u32[]{:S(2)}, u32[]{:S(2)}) collective-permute-start(bf16[32,128,8]{1,2,0:T(8,128)(2,1)} %copy.35), channel_id=1, source_target_pairs={{0,2},{2,4},{4,6},{6,8},{8,10},{10,12},{12,14},{14,16},{16,18},{18... | collective-permute-start | bytes 196616 | tf_op jit(solution)/shard_map/ppermute | solution.py:17
  28.0 13.6 %collective-permute-start.3 = (bf16[32,128,8]{1,2,0:T(8,128)(2,1)S(1)}, bf16[32,128,8]{1,2,0:T(8,128)(2,1)}, u32[]{:S(2)}, u32[]{:S(2)}) collective-permute-start(bf16[32,128,8]{1,2,0:T(8,128)(2,1)S(1)} %copy.36), channel_id=1, source_target_pairs={{2,0},{4,2},{6,4},{8,6},{10,8},{12,10},{14,12},{16,14},{18,16},{20... | collective-permute-start | bytes 196616 | tf_op jit(solution)/shard_map/ppermute | solution.py:18
  47.5 2.4 copy-start.12
  49.9 3.4 copy-start.4
  53.3 9.2 %copy-start.2 = (bf16[32,96,128]{2,0,1:T(8,128)(2,1)}, bf16[32,96,128]{2,0,1:T(8,128)(2,1)S(1)}, u32[]{:S(2)}) copy-start(bf16[32,96,128]{2,0,1:T(8,128)(2,1)S(1)} %get-tuple-element.40) | copy-start | bytes 2359300
  53.3 8.6 %collective-permute-start.4 = (bf16[32,16,128]{2,0,1:T(8,128)(2,1)S(1)}, bf16[32,16,128]{2,0,1:T(8,128)(2,1)S(1)}, u32[]{:S(2)}, u32[]{:S(2)}) collective-permute-start(bf16[32,16,128]{2,0,1:T(8,128)(2,1)S(1)} %get-tuple-element.35), channel_id=1, source_target_pairs={{0,1},{2,3},{4,5},{6,7},{8,9},{10,11},{12,13},{14,15},{16,17},{18,... | collective-permute-start | bytes 393224 | tf_op jit(solution)/shard_map/ppermute | solution.py:17
  54.6 7.3 %collective-permute-start.5 = (bf16[32,16,128]{2,0,1:T(8,128)(2,1)S(1)}, bf16[32,16,128]{2,0,1:T(8,128)(2,1)S(1)}, u32[]{:S(2)}, u32[]{:S(2)}) collective-permute-start(bf16[32,16,128]{2,0,1:T(8,128)(2,1)S(1)} %get-tuple-element.36), channel_id=1, source_target_pairs={{1,0},{3,2},{5,4},{7,6},{9,8},{11,10},{13,12},{15,14},{17,16},{19,... | collective-permute-start | bytes 393224 | tf_op jit(solution)/shard_map/ppermute | solution.py:18
  56.6 15.8 %collective-permute-start.8 = (bf16[32,16,128]{2,0,1:T(8,128)(2,1)}, bf16[32,16,128]{2,0,1:T(8,128)(2,1)S(1)}, u32[]{:S(2)}, u32[]{:S(2)}) collective-permute-start(bf16[32,16,128]{2,0,1:T(8,128)(2,1)} %get-tuple-element.33), channel_id=1, source_target_pairs={{0,1},{2,3},{4,5},{6,7},{8,9},{10,11},{12,13},{14,15},{16,17},{18,... | collective-permute-start | bytes 393224 | tf_op jit(solution)/shard_map/ppermute | solution.py:17
  60.6 11.8 %collective-permute-start.9 = (bf16[32,16,128]{2,0,1:T(8,128)(2,1)}, bf16[32,16,128]{2,0,1:T(8,128)(2,1)S(1)}, u32[]{:S(2)}, u32[]{:S(2)}) collective-permute-start(bf16[32,16,128]{2,0,1:T(8,128)(2,1)} %get-tuple-element.34), channel_id=1, source_target_pairs={{1,0},{3,2},{5,4},{7,6},{9,8},{11,10},{13,12},{15,14},{17,16},{19,... | collective-permute-start | bytes 393224 | tf_op jit(solution)/shard_map/ppermute | solution.py:18
  64.2 17.7 %collective-permute-start.6 = (bf16[32,128,8]{1,2,0:T(8,128)(2,1)}, bf16[32,128,8]{1,2,0:T(8,128)(2,1)}, u32[]{:S(2)}, u32[]{:S(2)}) collective-permute-start(bf16[32,128,8]{1,2,0:T(8,128)(2,1)} %copy.41), channel_id=1, source_target_pairs={{0,2},{2,4},{4,6},{6,8},{8,10},{10,12},{12,14},{14,16},{16,18},{18... | collective-permute-start | bytes 196616 | tf_op jit(solution)/shard_map/ppermute | solution.py:17
  70.5 14.6 %collective-permute-start.7 = (bf16[32,128,8]{1,2,0:T(8,128)(2,1)}, bf16[32,128,8]{1,2,0:T(8,128)(2,1)}, u32[]{:S(2)}, u32[]{:S(2)}) collective-permute-start(bf16[32,128,8]{1,2,0:T(8,128)(2,1)} %copy.42), channel_id=1, source_target_pairs={{2,0},{4,2},{6,4},{8,6},{10,8},{12,10},{14,12},{16,14},{18,16},{20... | collective-permute-start | bytes 196616 | tf_op jit(solution)/shard_map/ppermute | solution.py:18
  74.6 19.4 %collective-permute-start.10 = (bf16[32,128,8]{1,2,0:T(8,128)(2,1)}, bf16[32,128,8]{1,2,0:T(8,128)(2,1)}, u32[]{:S(2)}, u32[]{:S(2)}) collective-permute-start(bf16[32,128,8]{1,2,0:T(8,128)(2,1)} %copy.48), channel_id=1, source_target_pairs={{0,2},{2,4},{4,6},{6,8},{8,10},{10,12},{12,14},{14,16},{16,18},{18... | collective-permute-start | bytes 196616 | tf_op jit(solution)/shard_map/ppermute | solution.py:17
  80.0 17.2 %collective-permute-start.11 = (bf16[32,128,8]{1,2,0:T(8,128)(2,1)}, bf16[32,128,8]{1,2,0:T(8,128)(2,1)}, u32[]{:S(2)}, u32[]{:S(2)}) collective-permute-start(bf16[32,128,8]{1,2,0:T(8,128)(2,1)} %copy.49), channel_id=1, source_target_pairs={{2,0},{4,2},{6,4},{8,6},{10,8},{12,10},{14,12},{16,14},{18,16},{20... | collective-permute-start | bytes 196616 | tf_op jit(solution)/shard_map/ppermute | solution.py:18
  105.7 3.2 copy-start.8
  105.7 3.1 copy-start.16
  107.2 4.2 slice-start
  108.9 2.4 slice-start.1
  111.3 2.8 copy-start
  111.3 4.0 copy-start.3
  121.5 11.4 %copy-start.6 = (bf16[32,96,128]{2,1,0:T(8,128)(2,1)S(1)}, bf16[32,96,128]{2,1,0:T(8,128)(2,1)}, u32[]{:S(2)}) copy-start(bf16[32,96,128]{2,1,0:T(8,128)(2,1)} %param.7) | copy-start | bytes 2359300
  127.3 266.5 %collective-permute-start.12 = (bf16[32,16,128]{2,0,1:T(8,128)(2,1)S(1)}, bf16[32,16,128]{2,0,1:T(8,128)(2,1)S(1)}, u32[]{:S(2)}, u32[]{:S(2)}) collective-permute-start(bf16[32,16,128]{2,0,1:T(8,128)(2,1)S(1)} %get-tuple-element.31), channel_id=1, source_target_pairs={{0,1},{2,3},{4,5},{6,7},{8,9},{10,11},{12,13},{14,15},{16,17},{18,... | collective-permute-start | bytes 393224 | tf_op jit(solution)/shard_map/ppermute | solution.py:17
  131.6 262.2 %collective-permute-start.13 = (bf16[32,16,128]{2,0,1:T(8,128)(2,1)S(1)}, bf16[32,16,128]{2,0,1:T(8,128)(2,1)S(1)}, u32[]{:S(2)}, u32[]{:S(2)}) collective-permute-start(bf16[32,16,128]{2,0,1:T(8,128)(2,1)S(1)} %get-tuple-element.32), channel_id=1, source_target_pairs={{1,0},{3,2},{5,4},{7,6},{9,8},{11,10},{13,12},{15,14},{17,16},{19,... | collective-permute-start | bytes 393224 | tf_op jit(solution)/shard_map/ppermute | solution.py:18
  132.9 260.9 %copy-start.1 = (bf16[32,96,128]{2,0,1:T(8,128)(2,1)S(1)}, bf16[32,96,128]{2,0,1:T(8,128)(2,1)}, u32[]{:S(2)}) copy-start(bf16[32,96,128]{2,0,1:T(8,128)(2,1)} %copy-done) | copy-start | bytes 2359300
  393.8 10.1 %copy-start.15 = (f32[32]{0:T(128)S(1)}, f32[32]{0:T(128)}, u32[]{:S(2)}) copy-start(f32[32]{0:T(128)} %get-tuple-element.21) | copy-start | bytes 388
  397.5 8.7 %collective-permute-start.14 = (bf16[32,128,8]{1,2,0:T(8,128)(2,1)S(1)}, bf16[32,128,8]{1,2,0:T(8,128)(2,1)S(1)}, u32[]{:S(2)}, u32[]{:S(2)}) collective-permute-start(bf16[32,128,8]{1,2,0:T(8,128)(2,1)S(1)} %copy.53), channel_id=1, source_target_pairs={{0,2},{2,4},{4,6},{6,8},{8,10},{10,12},{12,14},{14,16},{16,18},{18... | collective-permute-start | bytes 196616 | tf_op jit(solution)/shard_map/ppermute | solution.py:17
  402.0 5.6 %collective-permute-start.15 = (bf16[32,128,8]{1,2,0:T(8,128)(2,1)S(1)}, bf16[32,128,8]{1,2,0:T(8,128)(2,1)S(1)}, u32[]{:S(2)}, u32[]{:S(2)}) collective-permute-start(bf16[32,128,8]{1,2,0:T(8,128)(2,1)S(1)} %copy.54), channel_id=1, source_target_pairs={{2,0},{4,2},{6,4},{8,6},{10,8},{12,10},{14,12},{16,14},{18,16},{20... | collective-permute-start | bytes 196616 | tf_op jit(solution)/shard_map/ppermute | solution.py:18
  (4 other events, 8.1 us)
Sparse Core Ops, SparseCore 0:
  133.0 259.1 all-reduce.2
where the time goes:
time: 435 us; the launch traced here: 427 us
  waiting for transfers between devices  258 us (59%)
  local copies, waits for them, and re-layouts  63.3 us (15%)
  starting transfers between devices  43.4 us (10%)
  between operations  24.1 us (6%)
  matrix products  21 us (5%)
  other arithmetic  17.1 us (4%)
    psum x1, waiting for transfers between devices, shards(): lax.psum((local_one, local_bias, local_two), ('bins', 'diag'))  253 us
    ppermute x8, starting transfers between devices, with_halo(): before = lax.ppermute(last, axis, up)  30.3 us
    unnamed x74, local copies, waits for them, and re-layouts  22.4 us
    ppermute x8, starting transfers between devices, with_halo(): after = lax.ppermute(initial, axis, down)  13.1 us
    dot_general x4, matrix products, apply_taps(): jnp.einsum('ok,kdi->odi', matrix, patches, preferred_element_type=jnp.flo...  12.5 us
    concatenate x8, other arithmetic, with_halo(): shard = jnp.concatenate([before, shard, after], axis=dim)  12 us
    ppermute x4, local copies, waits for them, and re-layouts, with_halo(): after = lax.ppermute(initial, axis, down)  10.9 us
    slice x12, local copies, waits for them, and re-layouts, with_halo(): last = lax.slice_in_dim(shard, length - width, length, axis=dim)  10.6 us
  transfers between devices with their start and end apart: 17, of which 3 were waited for; matrix products, arithmetic and copies ran while one was open for 9% of the time, Pallas kernels for 0%

commit v1 on v0

v1 whole, which is shorter than its diff:
```python
import jax
import jax.numpy as jnp
from jax import lax
from jax.experimental import pallas as pl
from jax.experimental.pallas import tpu as pltpu
from jax.sharding import PartitionSpec as P

F32, BF16 = jnp.float32, jnp.bfloat16
MESH = pl.DeviceIdType.MESH
C = 32
ROWS = 96
LANES = 128
HALO = 16
STRIP = 8
EXT = ROWS + 2 * HALO
CHUNKS = ROWS // HALO
NEAR = 8
GROUP = 16
PARTS = 10
CELLS = 3145728
TAPS = [(a, b) for a in (-1, 0, 1) for b in (-1, 0, 1)]
STEP = 4


def sigmoid(v):
    return 1.0 / (1.0 + jnp.exp(-v))


def kernel(
    rate, feat, cot, mask, w1, b1, w2,
    out, gfeat, g1, gb, g2,
    own, strips, shifted, maskf, slope, weights, wstage, bias, conv,
    got_d, got_i, got_c, sums, got, part, total,
    send_d, recv_d, send_i, recv_i, send_c, recv_c, send1, recv1, send2, recv2, send3, recv3,
):
    bins, diag = lax.axis_index("bins"), lax.axis_index("diag")
    count = lax.axis_size("bins")
    right, left = (bins + 1) % count, (bins + count - 1) % count
    across = 1 - diag
    near, far = (bins % NEAR) * 2 + diag, bins // NEAR

    def near_peer(step):
        rank = (near + step) % GROUP
        return rank, (far * NEAR + rank // 2, rank % 2)

    def far_peer(step):
        rank = (far + step) % GROUP
        return rank, (rank * NEAR + bins % NEAR, diag)

    peers = [near_peer(s)[1] for s in range(1, GROUP)] + [far_peer(s)[1] for s in range(1, GROUP)]
    peers += [(left, diag), (right, diag), (left, across), (right, across)]
    barrier = pltpu.get_barrier_semaphore()
    for peer in peers:
        pl.semaphore_signal(barrier, inc=1, device_id=peer, device_id_type=MESH)

    r1, r2 = rate[0], rate[1]
    lane = lax.broadcasted_iota(jnp.int32, (C, LANES), 1)
    edge_start = (ROWS - HALO) * (1 - diag)
    edge_chunk = (CHUNKS - 1) * (1 - diag)
    halo_start = (ROWS + HALO) * (1 - diag)
    zero_start = (ROWS + HALO) * diag

    maskf[...] = mask[...].astype(F32)

    def enter(q, _):
        rows = pl.ds(pl.multiple_of(q * HALO, HALO), HALO)
        m = maskf[rows, :][None]
        x = feat[:, rows, :].astype(F32)
        s = sigmoid(x)
        act = (x * s * m).astype(BF16)
        slope[:, rows, :] = m * s * (1.0 + x * (1.0 - s))
        own[0, rows] = jnp.transpose(act, (1, 0, 2))
        grad = (cot[:, rows, :].astype(F32) * m).astype(BF16)
        own[1, rows] = jnp.transpose(grad, (1, 0, 2))
        return 0

    lax.fori_loop(0, CHUNKS, enter, 0)

    def pack(field):
        def chunk(q, _):
            up = jnp.zeros((C, LANES), BF16)
            down = jnp.zeros((C, LANES), BF16)
            for j in range(HALO):
                row = own[field, q * HALO + j]
                inside = (lane >= STRIP * j) & (lane < STRIP * (j + 1))
                up = jnp.where(inside, pltpu.roll(row, (STRIP * (j + 1)) % LANES, 1), up)
                down = jnp.where(inside, pltpu.roll(row, STRIP * j, 1), down)
            strips[0, field, q] = up
            strips[1, field, q] = down
            return 0

        lax.fori_loop(0, CHUNKS, chunk, 0)

    def exchange(rnd):
        two = pl.ds(2 * rnd, 2)
        copies = [
            pltpu.make_async_remote_copy(
                src_ref=own.at[two, pl.ds(edge_start, HALO)], dst_ref=got_d.at[rnd],
                send_sem=send_d.at[rnd], recv_sem=recv_d.at[rnd],
                device_id=(bins, across), device_id_type=MESH)
        ]
        for side, to in enumerate((right, left)):
            copies.append(
                pltpu.make_async_remote_copy(
                    src_ref=strips.at[side, two], dst_ref=got_i.at[rnd, side],
                    send_sem=send_i.at[rnd, side], recv_sem=recv_i.at[rnd, side],
                    device_id=(to, diag), device_id_type=MESH))
            copies.append(
                pltpu.make_async_remote_copy(
                    src_ref=strips.at[side, two, edge_chunk], dst_ref=got_c.at[rnd, side],
                    send_sem=send_c.at[rnd, side], recv_sem=recv_c.at[rnd, side],
                    device_id=(to, across), device_id_type=MESH))
        return copies

    def clear_ends(rnd):
        for side, end in ((0, 0), (1, count - 1)):
            @pl.when(bins == end)
            def _():
                got_i[rnd, side] = jnp.zeros(got_i.shape[2:], BF16)
                got_c[rnd, side] = jnp.zeros(got_c.shape[2:], BF16)

    def shift_rows(row_of, before, after, r, store):
        for j in range(HALO):
            row = row_of(j)
            low = pltpu.roll(before, (r - STRIP * (j + 1) + LANES) % LANES, 1)
            high = pltpu.roll(after, (2 * LANES - r - STRIP * j) % LANES, 1)
            store(j, 0, jnp.where(lane < r, low, pltpu.roll(row, r, 1)))
            store(j, 1, row)
            store(j, 2, jnp.where(lane >= LANES - r, high, pltpu.roll(row, LANES - r, 1)))

    def shift(field, r):
        rnd, slot = field // 2, field % 2

        def chunk(q, _):
            def store(j, a, value):
                shifted[field, a, HALO + q * HALO + j] = value

            shift_rows(lambda j: own[field, q * HALO + j], got_i[rnd, 0, slot, q],
                       got_i[rnd, 1, slot, q], r, store)
            return 0

        lax.fori_loop(0, CHUNKS, chunk, 0)

        def store(j, a, value):
            shifted[field, a, halo_start + j] = value

        shift_rows(lambda j: got_d[rnd, slot, j], got_c[rnd, 0, slot], got_c[rnd, 1, slot], r, store)
        for a in range(3):
            shifted[field, a, pl.ds(zero_start, HALO)] = jnp.zeros((HALO, C, LANES), BF16)

    def patches(field, r, sign, d, step):
        blocks = []
        for a, b in TAPS:
            start = HALO + d + sign * (b - a) * r
            blocks.append(
                jnp.concatenate([shifted[field, sign * a + 1, start + j] for j in range(step)], axis=1)
            )
        return jnp.concatenate(blocks, axis=0)

    pack(0)
    pack(1)
    pl.semaphore_wait(barrier, len(peers))
    first = exchange(0)
    for copy in first:
        copy.start()

    bias[...] = jnp.broadcast_to(jnp.transpose(jnp.broadcast_to(b1[...], (C, C)))[:, :1], (C, LANES))
    for k, ref in enumerate((w1, w2)):
        wstage[...] = ref[...].astype(F32)
        taps = [wstage[:, t, :] for t in range(9)]
        weights[2 * k] = jnp.concatenate(taps, axis=1).astype(BF16)
        weights[2 * k + 1] = jnp.concatenate([jnp.transpose(t) for t in taps], axis=1).astype(BF16)

    for copy in first:
        copy.wait()
    clear_ends(0)
    shift(0, r1)
    shift(1, r2)

    def middle(n, _):
        d = n * STEP
        pre = jnp.dot(weights[0], patches(0, r1, 1, d, STEP), preferred_element_type=F32)
        back = jnp.dot(weights[3], patches(1, r2, -1, d, STEP), preferred_element_type=F32)
        for j in range(STEP):
            m = maskf[pl.ds(d + j, 1), :]
            y = pre[:, j * LANES : (j + 1) * LANES] + bias[...]
            s = sigmoid(y)
            own[2, d + j] = (y * s * m).astype(BF16)
            grad = back[:, j * LANES : (j + 1) * LANES] * m * (s * (1.0 + y * (1.0 - s)))
            own[3, d + j] = grad.astype(BF16)
        return 0

    lax.fori_loop(0, ROWS // STEP, middle, 0, unroll=2)

    pack(2)
    pack(3)
    second = exchange(1)
    for copy in second:
        copy.start()

    wide = 16

    def grads(n, carry):
        d = n * wide
        upstream = jnp.concatenate([own[3, d + j] for j in range(wide)], axis=1)
        hidden = jnp.concatenate([own[2, d + j] for j in range(wide)], axis=1)
        nt = (((1,), (1,)), ((), ()))
        one = lax.dot_general(patches(0, r1, 1, d, wide), upstream, nt, preferred_element_type=F32)
        two = lax.dot_general(patches(1, r2, -1, d, wide), hidden, nt, preferred_element_type=F32)
        ones = jnp.ones((16, wide * LANES), BF16)
        total_b = lax.dot_general(ones, upstream, nt, preferred_element_type=F32)
        return carry[0] + one, carry[1] + two, carry[2] + total_b

    zero = jnp.zeros((9 * C, C), F32)
    one, two, bias_sum = lax.fori_loop(0, ROWS // wide, grads, (zero, zero, jnp.zeros((16, C), F32)))
    for k, value in enumerate((one, two)):
        wide4 = jnp.concatenate([value[2 * C * g : 2 * C * (g + 1)] for g in range(4)], axis=1)
        for p in range(4):
            sums[4 * k + p] = wide4[HALO * p : HALO * (p + 1)]
    last = [one[8 * C :], two[8 * C :], jnp.concatenate([bias_sum, jnp.zeros((16, C), F32)], axis=0)]
    last = jnp.concatenate(last + [jnp.zeros((C, C), F32)], axis=1)
    sums[8] = last[:HALO]
    sums[9] = last[HALO:]

    def scatter(step):
        rank, device = near_peer(step)
        return rank, pltpu.make_async_remote_copy(
            src_ref=sums.at[rank % PARTS], dst_ref=got.at[step], send_sem=send1.at[step],
            recv_sem=recv1.at[step], device_id=device, device_id_type=MESH)

    for step in range(1, GROUP):
        rank, copy = scatter(step)
        pl.when(rank < PARTS)(copy.start)

    for copy in second:
        copy.wait()
    clear_ends(1)
    shift(2, r2)

    def forward(n, _):
        d = n * STEP
        y = jnp.dot(weights[2], patches(2, r2, 1, d, STEP), preferred_element_type=F32)
        for j in range(STEP):
            conv[d + j] = y[:, j * LANES : (j + 1) * LANES]
        return 0

    lax.fori_loop(0, ROWS // STEP, forward, 0, unroll=2)

    def finish_forward(q, _):
        rows = pl.ds(pl.multiple_of(q * HALO, HALO), HALO)
        y = jnp.transpose(conv[rows], (1, 0, 2))
        out[:, rows, :] = (feat[:, rows, :].astype(F32) + maskf[rows, :][None] * y).astype(BF16)
        return 0

    lax.fori_loop(0, CHUNKS, finish_forward, 0)

    for step in range(1, GROUP):
        rank, copy = scatter(step)
        pl.when(rank < PARTS)(copy.wait_send)

    spread = []
    for step in range(1, GROUP):
        rank, device = far_peer(step)
        spread.append(pltpu.make_async_remote_copy(
            src_ref=part.at[far], dst_ref=part.at[far], send_sem=send2.at[step],
            recv_sem=recv2.at[step], device_id=device, device_id_type=MESH))

    @pl.when(near < PARTS)
    def _():
        value = sums[near % PARTS]
        for step in range(1, GROUP):
            scatter(step)[1].wait_recv()
            value = value + got[step]
        part[far] = value
        for copy in spread:
            copy.start()

    shift(3, r1)

    def backward(n, _):
        d = n * STEP
        y = jnp.dot(weights[1], patches(3, r1, -1, d, STEP), preferred_element_type=F32)
        for j in range(STEP):
            conv[d + j] = y[:, j * LANES : (j + 1) * LANES]
        return 0

    lax.fori_loop(0, ROWS // STEP, backward, 0, unroll=2)

    def finish_backward(q, _):
        rows = pl.ds(pl.multiple_of(q * HALO, HALO), HALO)
        y = jnp.transpose(conv[rows], (1, 0, 2))
        gfeat[:, rows, :] = (cot[:, rows, :].astype(F32) + slope[:, rows, :] * y).astype(BF16)
        return 0

    lax.fori_loop(0, CHUNKS, finish_backward, 0)

    def gather(step):
        return near_peer(step)[0], pltpu.make_async_remote_copy(
            src_ref=total.at[near % PARTS], dst_ref=total.at[near % PARTS], send_sem=send3.at[step],
            recv_sem=recv3.at[step], device_id=near_peer(step)[1], device_id_type=MESH)

    @pl.when(near < PARTS)
    def _():
        for copy in spread:
            copy.wait_recv()
        value = part[0]
        for rank in range(1, GROUP):
            value = value + part[rank]
        total[near % PARTS] = value
        for step in range(1, GROUP):
            gather(step)[1].start()
        for copy in spread:
            copy.wait_send()
        for step in range(1, GROUP):
            gather(step)[1].wait_send()

    for step in range(1, GROUP):
        sender = (near - step + GROUP) % GROUP
        pl.when(sender < PARTS)(gather(step)[1].wait_recv)

    factor = 1.0 / jnp.sqrt(jnp.float32(CELLS))
    last = jnp.concatenate([total[8], total[9]], axis=0) * factor
    for k, ref in enumerate((g1, g2)):
        body = jnp.concatenate([total[4 * k + p] for p in range(4)], axis=0) * factor
        for t in range(9):
            if t < 8:
                block = body[(t % 2) * C : (t % 2 + 1) * C, (t // 2) * C : (t // 2 + 1) * C]
            else:
                block = last[:, k * C : (k + 1) * C]
            ref[:, t, :] = jnp.transpose(block) if k == 0 else block
    gb[...] = last[:1, 2 * C : 3 * C]


def shards(features, cotangent, band_mask, dilation, w_first, b_first, w_second):
    vmem = pl.BlockSpec(memory_space=pltpu.VMEM)
    dma = pltpu.SemaphoreType.DMA
    shape = jax.ShapeDtypeStruct
    field = (C, ROWS, LANES)
    taps = (C, 9, C)
    out, gfeat, g1, gb, g2 = pl.pallas_call(
        kernel,
        out_shape=[shape(field, BF16), shape(field, BF16), shape(taps, F32), shape((1, C), F32), shape(taps, F32)],
        in_specs=[pl.BlockSpec(memory_space=pltpu.SMEM)] + [vmem] * 6,
        out_specs=[vmem] * 5,
        scratch_shapes=[
            pltpu.VMEM((4, ROWS, C, LANES), BF16),
            pltpu.VMEM((2, 4, CHUNKS, C, LANES), BF16),
            pltpu.VMEM((4, 3, EXT, C, LANES), BF16),
            pltpu.VMEM((ROWS, LANES), F32),
            pltpu.VMEM(field, F32),
            pltpu.VMEM((4, C, 9 * C), BF16),
            pltpu.VMEM(taps, F32),
            pltpu.VMEM((C, LANES), F32),
            pltpu.VMEM((ROWS, C, LANES), F32),
            pltpu.VMEM((2, 2, HALO, C, LANES), BF16),
            pltpu.VMEM((2, 2, 2, CHUNKS, C, LANES), BF16),
            pltpu.VMEM((2, 2, 2, C, LANES), BF16),
            pltpu.VMEM((PARTS, HALO, LANES), F32),
            pltpu.VMEM((GROUP, HALO, LANES), F32),
            pltpu.VMEM((GROUP, HALO, LANES), F32),
            pltpu.VMEM((PARTS, HALO, LANES), F32),
            dma((2,)), dma((2,)), dma((2, 2)), dma((2, 2)), dma((2, 2)), dma((2, 2)),
            dma((GROUP,)), dma((GROUP,)), dma((GROUP,)), dma((GROUP,)), dma((GROUP,)), dma((GROUP,)),
        ],
        compiler_params=pltpu.CompilerParams(
            collective_id=0, has_side_effects=True, vmem_limit_bytes=48 * 1024 * 1024
        ),
    )(dilation, features, cotangent, band_mask, w_first, b_first[None], w_second)
    return (out, gfeat, g1, gb[0], g2)


def solution(mesh):
    field, whole = P(None, "diag", "bins"), P()
    return jax.shard_map(
        shards, mesh=mesh, in_specs=(field, field, P("diag", "bins"), whole, whole, whole, whole),
        out_specs=(field, field, whole, whole, whole), check_vma=False)
```

time: 435 us -> 64.7 us (0.15); the launches traced: 427 us -> 64.4 us
  waiting for transfers between devices: 258 us -> 0 us
  Pallas kernels: 0 us -> 56 us
  local copies, waits for them, and re-layouts: 63.3 us -> 7.68 us
  starting transfers between devices: 43.4 us -> 0 us
  between operations: 24.1 us -> 0.7 us
  matrix products: 21 us -> 0 us
  other arithmetic: 17.1 us -> 0 us
    psum x1 -> x0, waiting for transfers between devices: 253 us -> none  [shards(): lax.psum((local_one, local_bias, local_two), ('bins', 'diag'))]
    pallas_call x0 -> x1, Pallas kernels: none -> 56 us  [shards(): pl.pallas_call(kernel, out_shape=[shape(field, BF16), shape(field, BF16),...]
    ppermute x16 -> x0, starting transfers between devices: 43.4 us -> none  [the longest x8 30.3 us: with_halo(): before = lax.ppermute(last, axis, up)]
    dot_general x6 -> x0, matrix products: 21 us -> none  [the longest x4 12.5 us: apply_taps(): jnp.einsum('ok,kdi->odi', matrix, patches, preferred_element_type=jnp.flo...]
    ppermute x8 -> x0, local copies, waits for them, and re-layouts: 20.2 us -> none  [the longest x4 10.9 us: with_halo(): after = lax.ppermute(initial, axis, down)]
    slice x17 -> x0, local copies, waits for them, and re-layouts: 16.7 us -> none  [the longest x12 10.6 us: with_halo(): last = lax.slice_in_dim(shard, length - width, length, axis=dim)]
    unnamed x74 -> x19, local copies, waits for them, and re-layouts: 22.4 us -> 7.68 us
    concatenate x8 -> x0, other arithmetic: 12 us -> none  [with_halo(): shard = jnp.concatenate([before, shard, after], axis=dim)]
  transfers between devices with their start and end apart: 17 -> 0, of which waited for: 3 -> 0; matrix products, arithmetic and copies ran while one was open for 9% -> 0% of each run, Pallas kernels for 0% -> 0%
where the time goes in v1:
time: 64.7 us; the launch traced here: 64.4 us
  Pallas kernels  56 us (87%)
  local copies, waits for them, and re-layouts  7.68 us (12%)
  between operations  0.7 us (1%)
    pallas_call x1, Pallas kernels, shards(): pl.pallas_call(kernel, out_shape=[shape(field, BF16), shape(field, BF16),...  56 us
    unnamed x19, local copies, waits for them, and re-layouts  7.68 us

profile of v1, /device:TPU:1, one launch (start us, length us, event | category | flops | bytes accessed | tf_op | source)
XLA Modules:
  0.0 64.4 jit_solution(10708107858376282271)
XLA Ops:
  0.6 0.0 copy-start.5
  0.6 1.0 %copy.12.w1 = bf16[32,9,32]{2,1,0:T(8,128)(2,1)S(1)} copy(bf16[32,9,32]{2,0,1:T(8,128)(2,1)} %param.11) | data formatting | bytes 36864 | tf_op args[4]
  1.6 0.0 copy-done.5
  1.6 0.0 copy-start.2
  1.6 0.0 copy-start.3
  1.6 0.0 copy-start.4
  1.7 0.7 %copy-done.2 = s32[96,128]{1,0:T(8,128)S(1)} copy-done((s32[96,128]{1,0:T(8,128)S(1)}, s32[96,128]{1,0:T(8,128)}, u32[]{:S(2)}) %copy-start.2) | copy-done | bytes 49176
  2.4 0.0 copy-done.3
  2.4 0.0 copy-done.4
  2.4 0.0 copy-start
  2.4 1.1 %copy-done = bf16[32,96,128]{2,1,0:T(8,128)(2,1)S(1)} copy-done((bf16[32,96,128]{2,1,0:T(8,128)(2,1)S(1)}, bf16[32,96,128]{2,1,0:T(8,128)(2,1)}, u32[]{:S(2)}) %copy-start) | copy-done | bytes 786456
  3.6 0.0 copy-start.1
  3.6 1.1 %copy-done.1 = bf16[32,96,128]{2,1,0:T(8,128)(2,1)S(1)} copy-done((bf16[32,96,128]{2,1,0:T(8,128)(2,1)S(1)}, bf16[32,96,128]{2,1,0:T(8,128)(2,1)}, u32[]{:S(2)}) %copy-start.1) | copy-done | bytes 786456
  4.7 56.0 %shard_map.110 = (bf16[32,96,128]{2,1,0:T(8,128)(2,1)S(1)}, bf16[32,96,128]{2,1,0:T(8,128)(2,1)S(1)}, f32[32,9,32]{2,1,0:T(8,128)S(1)}, f32[1,32]{1,0:T(1,128)S(1)}, f32[32,9,32]{2,1,0:T(8,128)S(1)}) custom-call(s32[2]{0:T(128)S(1)} %copy-done.3, bf16[32,96,128]{2,1,0:T(8,128)(2,1)S(1)} %copy-done, bf16[32,96,128]{2,1,0:T(8,128)(2,1)S(1)} %copy-done.1, ...), custom_call_target="tpu_custom_call" | custom-call | tf_op jit(solution)/shard_map/pallas_call | solution.py:340
  60.7 0.7 %copy.14 = f32[32,9,32]{2,0,1:T(8,128)} copy(f32[32,9,32]{2,1,0:T(8,128)S(1)} %get-tuple-element.17) | data formatting | bytes 73728
  61.4 0.7 %copy.15 = f32[32,9,32]{2,0,1:T(8,128)} copy(f32[32,9,32]{2,1,0:T(8,128)S(1)} %get-tuple-element.19) | data formatting | bytes 73728
  62.1 0.9 %copy.19 = bf16[32,96,128]{2,1,0:T(8,128)(2,1)} copy(bf16[32,96,128]{2,1,0:T(8,128)(2,1)S(1)} %get-tuple-element.25) | data formatting | bytes 1572864
  63.0 0.9 %copy.20 = bf16[32,96,128]{2,1,0:T(8,128)(2,1)} copy(bf16[32,96,128]{2,1,0:T(8,128)(2,1)S(1)} %get-tuple-element.26) | data formatting | bytes 1572864
  63.9 0.5 copy.21
  (1 shorter events, 0.0 us)
Async XLA Ops:
  0.6 1.0 %copy-start.5 = (bf16[32,9,32]{2,0,1:T(8,128)(2,1)S(1)}, bf16[32,9,32]{2,0,1:T(8,128)(2,1)}, u32[]{:S(2)}) copy-start(bf16[32,9,32]{2,0,1:T(8,128)(2,1)} %param.13) | copy-start | bytes 55300
  1.6 0.8 %copy-start.2 = (s32[96,128]{1,0:T(8,128)S(1)}, s32[96,128]{1,0:T(8,128)}, u32[]{:S(2)}) copy-start(s32[96,128]{1,0:T(8,128)} %mask.1) | copy-start | bytes 147460
  1.6 0.8 %copy-start.3 = (s32[2]{0:T(128)S(1)}, s32[2]{0:T(128)}, u32[]{:S(2)}) copy-start(s32[2]{0:T(128)} %rate.1) | copy-start | bytes 28
  1.6 0.8 %copy-start.4 = (f32[32]{0:T(128)S(1)}, f32[32]{0:T(128)}, u32[]{:S(2)}) copy-start(f32[32]{0:T(128)} %param.12) | copy-start | bytes 388
  2.4 1.1 %copy-start = (bf16[32,96,128]{2,1,0:T(8,128)(2,1)S(1)}, bf16[32,96,128]{2,1,0:T(8,128)(2,1)}, u32[]{:S(2)}) copy-start(bf16[32,96,128]{2,1,0:T(8,128)(2,1)} %feat.1) | copy-start | bytes 2359300
  3.6 1.1 %copy-start.1 = (bf16[32,96,128]{2,1,0:T(8,128)(2,1)S(1)}, bf16[32,96,128]{2,1,0:T(8,128)(2,1)}, u32[]{:S(2)}) copy-start(bf16[32,96,128]{2,1,0:T(8,128)(2,1)} %cot.1) | copy-start | bytes 2359300

commit v2 on v1

v2 whole, which is shorter than its diff:
```python
import jax
import jax.numpy as jnp
from jax import lax
from jax.experimental import pallas as pl
from jax.experimental.pallas import tpu as pltpu
from jax.sharding import PartitionSpec as P

F32, BF16 = jnp.float32, jnp.bfloat16
MESH = pl.DeviceIdType.MESH
C = 32
ROWS = 96
LANES = 128
HALO = 16
STRIP = 8
EXT = ROWS + 2 * HALO
CHUNKS = ROWS // HALO
NEAR = 8
GROUP = 16
PARTS = 10
CELLS = 3145728
PAD = 2 * HALO
LAGS = (-2, -1, 0, 1, 2)
TAPS = [(a, b) for a in (-1, 0, 1) for b in (-1, 0, 1)]
STEP = 4


def sigmoid(v):
    return 0.5 + 0.5 * jnp.tanh(0.5 * v)


def kernel(
    rate, feat_in, cot_in, mask_in, w1_in, b1_in, w2_in,
    out_hbm, gfeat_hbm, g1, gb, g2,
    out, gfeat, feat, cot, mask, w1, b1, w2, own, padded, strips, shifted, maskf, weights, bias, conv,
    got_d, got_i, got_c, sums, got, part, total, load,
    send_d, recv_d, send_i, recv_i, send_c, recv_c, send1, recv1, send2, recv2, send3, recv3,
):
    bins, diag = lax.axis_index("bins"), lax.axis_index("diag")
    count = lax.axis_size("bins")
    right, left = (bins + 1) % count, (bins + count - 1) % count
    across = 1 - diag
    near, far = (bins % NEAR) * 2 + diag, bins // NEAR

    def near_peer(step):
        rank = (near + step) % GROUP
        return rank, (far * NEAR + rank // 2, rank % 2)

    def far_peer(step):
        rank = (far + step) % GROUP
        return rank, (rank * NEAR + bins % NEAR, diag)

    peers = [near_peer(s)[1] for s in range(1, GROUP)] + [far_peer(s)[1] for s in range(1, GROUP)]
    peers += [(left, diag), (right, diag), (left, across), (right, across)]
    barrier = pltpu.get_barrier_semaphore()
    for peer in peers:
        pl.semaphore_signal(barrier, inc=1, device_id=peer, device_id_type=MESH)

    r1, r2 = rate[0], rate[1]
    lane = lax.broadcasted_iota(jnp.int32, (C, LANES), 1)
    edge_start = (ROWS - HALO) * (1 - diag)
    edge_chunk = (CHUNKS - 1) * (1 - diag)
    halo_start = (ROWS + HALO) * (1 - diag)
    zero_start = (ROWS + HALO) * diag

    edge = pl.ds(pl.multiple_of(edge_start, HALO), HALO)
    rest = pl.ds(pl.multiple_of(HALO * diag, HALO), ROWS - HALO)
    loads = [
        pltpu.make_async_copy(src, dst, load.at[k])
        for k, (src, dst) in enumerate((
            (mask_in, mask),
            (feat_in.at[:, edge], feat.at[:, edge]),
            (cot_in.at[:, edge], cot.at[:, edge]),
            (feat_in.at[:, rest], feat.at[:, rest]),
            (cot_in.at[:, rest], cot.at[:, rest]),
            (w1_in, w1),
            (w2_in, w2),
            (b1_in, b1),
        ))
    ]
    for copy in loads:
        copy.start()
    for field in (0, 1):
        padded[field, :PAD] = jnp.zeros((PAD, C, LANES), BF16)
        padded[field, PAD + ROWS :] = jnp.zeros((PAD, C, LANES), BF16)
    for field in range(4):
        for a in range(3):
            shifted[field, a, pl.ds(zero_start, HALO)] = jnp.zeros((HALO, C, LANES), BF16)
    loads[0].wait()
    maskf[...] = mask[...].astype(F32)

    def enter(q):
        rows = pl.ds(pl.multiple_of(q * HALO, HALO), HALO)
        m = maskf[rows, :][None]
        x = feat[:, rows, :].astype(F32)
        own[0, rows] = jnp.transpose((x * sigmoid(x) * m).astype(BF16), (1, 0, 2))
        grad = (cot[:, rows, :].astype(F32) * m).astype(BF16)
        own[1, rows] = jnp.transpose(grad, (1, 0, 2))

    def pack(field):
        def chunk(q, _):
            up = jnp.zeros((C, LANES), BF16)
            down = jnp.zeros((C, LANES), BF16)
            for j in range(HALO):
                row = row_of(field, q * HALO + j)
                inside = (lane >= STRIP * j) & (lane < STRIP * (j + 1))
                up = jnp.where(inside, pltpu.roll(row, (STRIP * (j + 1)) % LANES, 1), up)
                down = jnp.where(inside, pltpu.roll(row, STRIP * j, 1), down)
            strips[0, field, q] = up
            strips[1, field, q] = down
            return 0

        lax.fori_loop(0, CHUNKS, chunk, 0)

    def edges(rnd, src):
        return pltpu.make_async_remote_copy(
            src_ref=src, dst_ref=got_d.at[rnd], send_sem=send_d.at[rnd], recv_sem=recv_d.at[rnd],
            device_id=(bins, across), device_id_type=MESH)

    def sides(field):
        copies = []
        for side, to in enumerate((right, left)):
            copies.append(
                pltpu.make_async_remote_copy(
                    src_ref=strips.at[side, field], dst_ref=got_i.at[side, field],
                    send_sem=send_i.at[side, field], recv_sem=recv_i.at[side, field],
                    device_id=(to, diag), device_id_type=MESH))
            copies.append(
                pltpu.make_async_remote_copy(
                    src_ref=strips.at[side, field, edge_chunk], dst_ref=got_c.at[side, field],
                    send_sem=send_c.at[side, field], recv_sem=recv_c.at[side, field],
                    device_id=(to, across), device_id_type=MESH))
        return copies

    def clear_ends(field):
        for side, end in ((0, 0), (1, count - 1)):
            @pl.when(bins == end)
            def _():
                got_i[side, field] = jnp.zeros(got_i.shape[2:], BF16)
                got_c[side, field] = jnp.zeros(got_c.shape[2:], BF16)

    def shift_rows(row_of, before, after, r, store):
        for j in range(HALO):
            row = row_of(j)
            low = pltpu.roll(before, (r - STRIP * (j + 1) + LANES) % LANES, 1)
            high = pltpu.roll(after, (2 * LANES - r - STRIP * j) % LANES, 1)
            store(j, 0, jnp.where(lane < r, low, pltpu.roll(row, r, 1)))
            store(j, 1, row)
            store(j, 2, jnp.where(lane >= LANES - r, high, pltpu.roll(row, LANES - r, 1)))

    def row_of(field, d):
        return own[field, d] if field < 2 else padded[field - 2, PAD + d]

    def shift(field, r):
        def chunk(q, _):
            def store(j, a, value):
                shifted[field, a, HALO + q * HALO + j] = value

            shift_rows(lambda j: row_of(field, q * HALO + j), got_i[0, field, q], got_i[1, field, q], r, store)
            return 0

        lax.fori_loop(0, CHUNKS, chunk, 0)

    def shift_halo(field, r):
        def store(j, a, value):
            shifted[field, a, halo_start + j] = value

        rows = got_d.at[field // 2, field % 2]
        shift_rows(lambda j: rows[j], got_c[0, field], got_c[1, field], r, store)

    def patches(field, r, sign, d, step):
        blocks = []
        for a, b in TAPS:
            start = HALO + d + sign * (b - a) * r
            blocks.append(
                jnp.concatenate([shifted[field, sign * a + 1, start + j] for j in range(step)], axis=1)
            )
        return jnp.concatenate(blocks, axis=0)

    loads[1].wait()
    loads[2].wait()
    enter(edge_chunk)
    pl.semaphore_wait(barrier, len(peers))
    edge_one = edges(0, own.at[:, edge])
    edge_one.start()
    loads[3].wait()
    loads[4].wait()

    def enter_rest(n, _):
        enter(n + diag)
        return 0

    lax.fori_loop(0, CHUNKS - 1, enter_rest, 0)
    pack(0)
    strips_a = sides(0)
    for copy in strips_a:
        copy.start()
    pack(1)
    strips_g = sides(1)
    for copy in strips_g:
        copy.start()

    for copy in loads[5:]:
        copy.wait()
    bias[...] = jnp.broadcast_to(jnp.transpose(jnp.broadcast_to(b1[...], (C, C)))[:, :1], (C, LANES))
    for k, ref in enumerate((w1, w2)):
        taps = [ref[t] for t in range(9)]
        weights[2 * k] = jnp.concatenate(taps, axis=1)
        weights[2 * k + 1] = jnp.concatenate(
            [jnp.transpose(t.astype(F32)).astype(BF16) for t in taps], axis=1)

    for copy in strips_a:
        copy.wait()
    clear_ends(0)
    shift(0, r1)
    for copy in strips_g:
        copy.wait()
    clear_ends(1)
    shift(1, r2)
    edge_one.wait()
    shift_halo(0, r1)
    shift_halo(1, r2)

    def middle(d):
        pre = jnp.dot(weights[0], patches(0, r1, 1, d, STEP), preferred_element_type=F32)
        back = jnp.dot(weights[3], patches(1, r2, -1, d, STEP), preferred_element_type=F32)
        for j in range(STEP):
            m = maskf[pl.ds(d + j, 1), :]
            y = pre[:, j * LANES : (j + 1) * LANES] + bias[...]
            s = sigmoid(y)
            padded[0, PAD + d + j] = (y * s * m).astype(BF16)
            grad = back[:, j * LANES : (j + 1) * LANES] * m * (s * (1.0 + y * (1.0 - s)))
            padded[1, PAD + d + j] = grad.astype(BF16)

    def middle_edge(n, _):
        middle(edge_start + n * STEP)
        return 0

    def middle_rest(n, _):
        middle(HALO * diag + n * STEP)
        return 0

    lax.fori_loop(0, HALO // STEP, middle_edge, 0, unroll=2)
    edge_two = edges(1, padded.at[:, pl.ds(PAD + edge_start, HALO)])
    edge_two.start()
    lax.fori_loop(0, (ROWS - HALO) // STEP, middle_rest, 0, unroll=2)

    wide = 16
    nt = (((1,), (1,)), ((), ()))

    def row_block(rows):
        return jnp.concatenate(rows, axis=1)

    def grads(n, carry):
        k = n * wide
        act = [row_block([shifted[0, a, k + j] for j in range(wide)]) for a in range(3)]
        act.append(jnp.ones((C, wide * LANES), BF16))
        ups = [row_block([padded[1, HALO + k - m * r1 + j] for j in range(wide)]) for m in LAGS]
        one = lax.dot_general(jnp.concatenate(ups, axis=0), jnp.concatenate(act, axis=0), nt,
                              preferred_element_type=F32)
        grad = [row_block([shifted[1, a, k + j] for j in range(wide)]) for a in range(3)]
        hid = [row_block([padded[0, HALO + k + m * r2 + j] for j in range(wide)]) for m in LAGS]
        two = lax.dot_general(jnp.concatenate(grad, axis=0), jnp.concatenate(hid, axis=0), nt,
                              preferred_element_type=F32)
        return carry[0] + one, carry[1] + two

    zero = (jnp.zeros((5 * C, 4 * C), F32), jnp.zeros((3 * C, 5 * C), F32))
    one, two = lax.fori_loop(0, EXT // wide, grads, zero)

    def block(value, i, j):
        return value[C * i : C * (i + 1), C * j : C * (j + 1)]

    blocks = [[block(one, b - a + 2, a + 1) for a, b in TAPS], [block(two, 1 - a, b - a + 2) for a, b in TAPS]]
    for k in range(2):
        for p in range(2):
            four = jnp.concatenate(blocks[k][4 * p : 4 * p + 4], axis=1)
            sums[4 * k + 2 * p] = four[:HALO]
            sums[4 * k + 2 * p + 1] = four[HALO:]
    four = jnp.concatenate([blocks[0][8], blocks[1][8], block(one, 2, 3), jnp.zeros((C, C), F32)], axis=1)
    sums[8] = four[:HALO]
    sums[9] = four[HALO:]

    def scatter(step):
        rank, device = near_peer(step)
        return rank, pltpu.make_async_remote_copy(
            src_ref=sums.at[rank % PARTS], dst_ref=got.at[step], send_sem=send1.at[step],
            recv_sem=recv1.at[step], device_id=device, device_id_type=MESH)

    for step in range(1, GROUP):
        rank, copy = scatter(step)
        pl.when(rank < PARTS)(copy.start)

    pack(2)
    strips_h = sides(2)
    for copy in strips_h:
        copy.start()
    pack(3)
    strips_q = sides(3)
    for copy in strips_q:
        copy.start()
    for copy in strips_h:
        copy.wait()
    clear_ends(2)
    shift(2, r2)
    edge_two.wait()
    shift_halo(2, r2)

    spread = []
    for step in range(1, GROUP):
        rank, device = far_peer(step)
        spread.append(pltpu.make_async_remote_copy(
            src_ref=part.at[far], dst_ref=part.at[far], send_sem=send2.at[step],
            recv_sem=recv2.at[step], device_id=device, device_id_type=MESH))

    @pl.when(near < PARTS)
    def _():
        value = sums[near % PARTS]
        for step in range(1, GROUP):
            scatter(step)[1].wait_recv()
            value = value + got[step]
        part[far] = value
        for copy in spread:
            copy.start()

    def forward(n, _):
        d = n * STEP
        y = jnp.dot(weights[2], patches(2, r2, 1, d, STEP), preferred_element_type=F32)
        for j in range(STEP):
            conv[d + j] = y[:, j * LANES : (j + 1) * LANES]
        return 0

    lax.fori_loop(0, ROWS // STEP, forward, 0, unroll=2)

    def finish_forward(q, _):
        rows = pl.ds(pl.multiple_of(q * HALO, HALO), HALO)
        y = jnp.transpose(conv[rows], (1, 0, 2))
        out[:, rows, :] = (feat[:, rows, :].astype(F32) + maskf[rows, :][None] * y).astype(BF16)
        return 0

    lax.fori_loop(0, CHUNKS, finish_forward, 0)
    store_out = pltpu.make_async_copy(out, out_hbm, load.at[0])
    store_out.start()
    for copy in strips_q:
        copy.wait()
    clear_ends(3)
    shift(3, r1)
    shift_halo(3, r1)

    def gather(step):
        return near_peer(step)[0], pltpu.make_async_remote_copy(
            src_ref=total.at[near % PARTS], dst_ref=total.at[near % PARTS], send_sem=send3.at[step],
            recv_sem=recv3.at[step], device_id=near_peer(step)[1], device_id_type=MESH)

    @pl.when(near < PARTS)
    def _():
        for copy in spread:
            copy.wait_recv()
        value = part[0]
        for rank in range(1, GROUP):
            value = value + part[rank]
        total[near % PARTS] = value
        for step in range(1, GROUP):
            gather(step)[1].start()

    def backward(n, _):
        d = n * STEP
        y = jnp.dot(weights[1], patches(3, r1, -1, d, STEP), preferred_element_type=F32)
        for j in range(STEP):
            conv[d + j] = y[:, j * LANES : (j + 1) * LANES]
        return 0

    lax.fori_loop(0, ROWS // STEP, backward, 0, unroll=2)

    def finish_backward(q, _):
        rows = pl.ds(pl.multiple_of(q * HALO, HALO), HALO)
        y = jnp.transpose(conv[rows], (1, 0, 2))
        x = feat[:, rows, :].astype(F32)
        s = sigmoid(x)
        slope = maskf[rows, :][None] * (s * (1.0 + x * (1.0 - s)))
        gfeat[:, rows, :] = (cot[:, rows, :].astype(F32) + slope * y).astype(BF16)
        return 0

    lax.fori_loop(0, CHUNKS, finish_backward, 0)
    store_gfeat = pltpu.make_async_copy(gfeat, gfeat_hbm, load.at[1])
    store_gfeat.start()
    for step in range(1, GROUP):
        rank, copy = scatter(step)
        pl.when(rank < PARTS)(copy.wait_send)

    @pl.when(near < PARTS)
    def _():
        for copy in spread:
            copy.wait_send()
        for step in range(1, GROUP):
            gather(step)[1].wait_send()

    for step in range(1, GROUP):
        sender = (near - step + GROUP) % GROUP
        pl.when(sender < PARTS)(gather(step)[1].wait_recv)

    factor = 1.0 / jnp.sqrt(jnp.float32(CELLS))
    last = jnp.concatenate([total[8], total[9]], axis=0) * factor
    for k, ref in enumerate((g1, g2)):
        for p in range(2):
            four = jnp.concatenate([total[4 * k + 2 * p], total[4 * k + 2 * p + 1]], axis=0) * factor
            for t in range(4):
                ref[4 * p + t] = four[:, C * t : C * (t + 1)]
        ref[8] = last[:, C * k : C * (k + 1)]
    gb[...] = jnp.transpose(last[:, 2 * C : 3 * C])[:1]
    store_out.wait()
    store_gfeat.wait()


def hand_over(*refs):
    given, results, held, sems = refs[:5], refs[5:10], refs[10:15], refs[15]
    loads = [pltpu.make_async_copy(given[k], held[k], sems.at[k]) for k in range(5)]
    stores = [pltpu.make_async_copy(held[k], results[k], sems.at[5 + k]) for k in range(5)]
    for copy in loads:
        copy.start()
    for load, store in zip(loads, stores):
        load.wait()
        store.start()
    for copy in stores:
        copy.wait()


def shards(features, cotangent, band_mask, dilation, w_first, b_first, w_second):
    vmem = pl.BlockSpec(memory_space=pltpu.VMEM)
    dma = pltpu.SemaphoreType.DMA
    shape = jax.ShapeDtypeStruct
    field = (C, ROWS, LANES)
    taps = (9, C, C)
    hbm = pl.BlockSpec(memory_space=pltpu.HBM)
    results = pl.pallas_call(
        kernel,
        out_shape=[shape(field, BF16), shape(field, BF16), shape(taps, F32), shape((1, C), F32), shape(taps, F32)],
        in_specs=[pl.BlockSpec(memory_space=pltpu.SMEM)] + [hbm] * 6,
        out_specs=[hbm] * 2 + [vmem] * 3,
        scratch_shapes=[
            pltpu.VMEM(field, BF16),
            pltpu.VMEM(field, BF16),
            pltpu.VMEM(field, BF16),
            pltpu.VMEM(field, BF16),
            pltpu.VMEM((ROWS, LANES), jnp.int32),
            pltpu.VMEM(taps, BF16),
            pltpu.VMEM((1, C), F32),
            pltpu.VMEM(taps, BF16),
            pltpu.VMEM((2, ROWS, C, LANES), BF16),
            pltpu.VMEM((2, ROWS + 2 * PAD, C, LANES), BF16),
            pltpu.VMEM((2, 4, CHUNKS, C, LANES), BF16),
            pltpu.VMEM((4, 3, EXT, C, LANES), BF16),
            pltpu.VMEM((ROWS, LANES), F32),
            pltpu.VMEM((4, C, 9 * C), BF16),
            pltpu.VMEM((C, LANES), F32),
            pltpu.VMEM((ROWS, C, LANES), F32),
            pltpu.VMEM((2, 2, HALO, C, LANES), BF16),
            pltpu.VMEM((2, 4, CHUNKS, C, LANES), BF16),
            pltpu.VMEM((2, 4, C, LANES), BF16),
            pltpu.VMEM((PARTS, HALO, LANES), F32),
            pltpu.VMEM((GROUP, HALO, LANES), F32),
            pltpu.VMEM((GROUP, HALO, LANES), F32),
            pltpu.VMEM((PARTS, HALO, LANES), F32),
            dma((8,)),
            dma((2,)), dma((2,)), dma((2, 4)), dma((2, 4)), dma((2, 4)), dma((2, 4)),
            dma((GROUP,)), dma((GROUP,)), dma((GROUP,)), dma((GROUP,)), dma((GROUP,)), dma((GROUP,)),
        ],
        compiler_params=pltpu.CompilerParams(
            collective_id=0, has_side_effects=True, vmem_limit_bytes=63 * 1024 * 1024
        ),
    )(dilation, features, cotangent, band_mask, jnp.transpose(w_first, (1, 0, 2)), b_first[None],
      jnp.transpose(w_second, (1, 0, 2)))
    out, gfeat, g1, gb, g2 = pl.pallas_call(
        hand_over,
        out_shape=[shape(r.shape, r.dtype) for r in results],
        in_specs=[hbm] * 5,
        out_specs=[hbm] * 5,
        scratch_shapes=[pltpu.VMEM(r.shape, r.dtype) for r in results] + [dma((10,))],
        compiler_params=pltpu.CompilerParams(vmem_limit_bytes=63 * 1024 * 1024),
    )(*results)
    return (out, gfeat, jnp.transpose(g1, (1, 0, 2)), gb[0], jnp.transpose(g2, (1, 0, 2)))


def solution(mesh):
    field, whole = P(None, "diag", "bins"), P()
    return jax.shard_map(
        shards, mesh=mesh, in_specs=(field, field, P("diag", "bins"), whole, whole, whole, whole),
        out_specs=(field, field, whole, whole, whole), check_vma=False)
```

time: 64.7 us -> 54.6 us (0.84)
  the two profiles are of different devices: /device:TPU:1 before, /device:TPU:4 now
where the time goes in v2:
time: 54.6 us; the launch traced here: 54.4 us
  Pallas kernels  53.8 us (99%)
  between operations  0.64 us (1%)
    pallas_call x1, Pallas kernels, shards(): pl.pallas_call(kernel, out_shape=[shape(field, BF16), shape(field, BF16),...  51.3 us
    pallas_call x1, Pallas kernels, shards(): pl.pallas_call(hand_over, out_shape=[shape(r.shape, r.dtype) for r in res...  2.45 us

profile of v2, /device:TPU:4, one launch (start us, length us, event | category | flops | bytes accessed | tf_op | source)
XLA Modules:
  0.0 54.4 jit_solution(6673104368885747081)
XLA Ops:
  0.6 51.3 %shard_map.110 = (bf16[32,96,128]{2,1,0:T(8,128)(2,1)}, bf16[32,96,128]{2,1,0:T(8,128)(2,1)}, f32[9,32,32]{2,1,0:T(8,128)}, f32[1,32]{1,0:T(1,128)}, f32[9,32,32]{2,1,0:T(8,128)}) custom-call(s32[2]{0:T(128)} %rate.1, bf16[32,96,128]{2,1,0:T(8,128)(2,1)} %feat_in.1, bf16[32,96,128]{2,1,0:T(8,128)(2,1)} %cot_in.1, s32[96,128]{1,0:T(8,128)} %mask_in.1, ...), custom_call_target="tpu_custom_call" | custom-call | tf_op jit(solution)/shard_map/pallas_call | solution.py:433
  52.0 2.5 %shard_map.111 = (bf16[32,96,128]{2,1,0:T(8,128)(2,1)}, bf16[32,96,128]{2,1,0:T(8,128)(2,1)}, f32[9,32,32]{2,1,0:T(8,128)}, f32[1,32]{1,0:T(1,128)}, f32[9,32,32]{2,1,0:T(8,128)}) custom-call(bf16[32,96,128]{2,1,0:T(8,128)(2,1)} %get-tuple-element.15.refs_0_, bf16[32,96,128]{2,1,0:T(8,128)(2,1)} %get-tuple-element.16.refs_1_, ...), custom_call_target="tpu_custom_call" | custom-call | tf_op jit(solution)/shard_map/pallas_call | solution.py:471

commit v3 on v2

v3 whole, which is shorter than its diff:
```python
import jax
import jax.numpy as jnp
from jax import lax
from jax.experimental import pallas as pl
from jax.experimental.pallas import tpu as pltpu
from jax.sharding import PartitionSpec as P

F32, BF16 = jnp.float32, jnp.bfloat16
MESH = pl.DeviceIdType.MESH
C = 32
ROWS = 96
LANES = 128
HALO = 16
STRIP = 8
EXT = ROWS + 2 * HALO
CHUNKS = ROWS // HALO
NEAR = 8
GROUP = 16
PART_ROWS = 10
CELLS = 3145728
PAD = 2 * HALO
LAGS = (-2, -1, 0, 1, 2)
ORDER = sorted(range(1, GROUP), key=lambda step: abs(step - GROUP // 2))
TAPS = [(a, b) for a in (-1, 0, 1) for b in (-1, 0, 1)]
SIDE = [(a, b) for a, b in TAPS if a]
CENTER = [(a, b) for a, b in TAPS if not a]
STEP = 4


def sigmoid(v):
    return 0.5 + 0.5 * jnp.tanh(0.5 * v)


def kernel(
    rate, feat_in, cot_in, mask_in, w1_in, b1_in, w2_in,
    out_hbm, gfeat_hbm, g1, gb, g2,
    out, gfeat, feat, cot, mask, w1, b1, w2, center, strips, side, maskf, w_side, w_center, bias, conv, conv_back,
    got_d, got_i, got_c, sums, got, part, total, load,
    send_d, recv_d, send_i, recv_i, send_c, recv_c, send1, recv1, send2, recv2, send3, recv3,
):
    bins, diag = lax.axis_index("bins"), lax.axis_index("diag")
    count = lax.axis_size("bins")
    right, left = (bins + 1) % count, (bins + count - 1) % count
    across = 1 - diag
    near, far = (bins % NEAR) * 2 + diag, bins // NEAR

    def near_peer(step):
        rank = (near + step) % GROUP
        return rank, (far * NEAR + rank // 2, rank % 2)

    def far_peer(step):
        rank = (far + step) % GROUP
        return rank, (rank * NEAR + bins % NEAR, diag)

    peers = [far_peer(s)[1] for s in ORDER] + [near_peer(s)[1] for s in ORDER]
    peers += [(left, diag), (right, diag), (left, across), (right, across)]
    barrier = pltpu.get_barrier_semaphore()
    for peer in peers:
        pl.semaphore_signal(barrier, inc=1, device_id=peer, device_id_type=MESH)

    r1, r2 = rate[0], rate[1]
    lane = lax.broadcasted_iota(jnp.int32, (C, LANES), 1)
    edge_start = (ROWS - HALO) * (1 - diag)
    edge_chunk = (CHUNKS - 1) * (1 - diag)
    halo_start = (ROWS + HALO) * (1 - diag)
    zero_start = (ROWS + HALO) * diag

    edge = pl.ds(pl.multiple_of(edge_start, HALO), HALO)
    rest = pl.ds(pl.multiple_of(HALO * diag, HALO), ROWS - HALO)
    loads = [
        pltpu.make_async_copy(src, dst, load.at[k])
        for k, (src, dst) in enumerate((
            (mask_in, mask),
            (feat_in.at[:, edge], feat.at[:, edge]),
            (cot_in.at[:, edge], cot.at[:, edge]),
            (feat_in.at[:, rest], feat.at[:, rest]),
            (cot_in.at[:, rest], cot.at[:, rest]),
            (w1_in, w1),
            (w2_in, w2),
            (b1_in, b1),
        ))
    ]
    for copy in loads:
        copy.start()
    for field in range(4):
        center[field, :PAD] = jnp.zeros((PAD, C, LANES), BF16)
        center[field, PAD + ROWS :] = jnp.zeros((PAD, C, LANES), BF16)
        for k in range(2):
            side[field, k, pl.ds(zero_start, HALO)] = jnp.zeros((HALO, C, LANES), BF16)
    loads[0].wait()
    maskf[...] = mask[...].astype(F32)

    def enter(q):
        rows = pl.ds(pl.multiple_of(q * HALO, HALO), HALO)
        m = maskf[rows, :][None]
        x = feat[:, rows, :].astype(F32)
        inner = pl.ds(pl.multiple_of(PAD + q * HALO, HALO), HALO)
        center[0, inner] = jnp.transpose((x * sigmoid(x) * m).astype(BF16), (1, 0, 2))
        grad = (cot[:, rows, :].astype(F32) * m).astype(BF16)
        center[1, inner] = jnp.transpose(grad, (1, 0, 2))

    def row_of(field, d):
        return center[field, PAD + d]

    def strip_copy(rnd, side, q):
        return pltpu.make_async_remote_copy(
            src_ref=strips.at[rnd, side, q], dst_ref=got_i.at[rnd, side, q],
            send_sem=send_i.at[rnd, side, q], recv_sem=recv_i.at[rnd, side, q],
            device_id=((right, left)[side], diag), device_id_type=MESH)

    def corner_copy(rnd, side):
        return pltpu.make_async_remote_copy(
            src_ref=strips.at[rnd, side, edge_chunk], dst_ref=got_c.at[rnd, side],
            send_sem=send_c.at[rnd, side], recv_sem=recv_c.at[rnd, side],
            device_id=((right, left)[side], across), device_id_type=MESH)

    def pack(rnd, q):
        for slot in range(2):
            up = jnp.zeros((C, LANES), BF16)
            down = jnp.zeros((C, LANES), BF16)
            for j in range(HALO):
                row = row_of(2 * rnd + slot, q * HALO + j)
                inside = (lane >= STRIP * j) & (lane < STRIP * (j + 1))
                up = jnp.where(inside, pltpu.roll(row, (STRIP * (j + 1)) % LANES, 1), up)
                down = jnp.where(inside, pltpu.roll(row, STRIP * j, 1), down)
            strips[rnd, 0, q, slot] = up
            strips[rnd, 1, q, slot] = down

    def order(n):
        return n + diag * (CHUNKS - 1 - 2 * n)

    def edge_copy(field):
        rnd, slot = field // 2, field % 2
        return pltpu.make_async_remote_copy(
            src_ref=center.at[field, pl.ds(PAD + edge_start, HALO)], dst_ref=got_d.at[rnd, slot],
            send_sem=send_d.at[rnd, slot], recv_sem=recv_d.at[rnd, slot],
            device_id=(bins, across), device_id_type=MESH)

    def settle(rnd, q):
        for side, end in ((0, 0), (1, count - 1)):
            strip_copy(rnd, side, q).wait_recv()

            @pl.when(bins == end)
            def _():
                got_i[rnd, side, q] = jnp.zeros((2, C, LANES), BF16)

    def settle_halo(rnd):
        edge_copy(2 * rnd).wait_recv()
        edge_copy(2 * rnd + 1).wait_recv()
        for side, end in ((0, 0), (1, count - 1)):
            corner_copy(rnd, side).wait_recv()

            @pl.when(bins == end)
            def _():
                got_c[rnd, side] = jnp.zeros((2, C, LANES), BF16)

    def shift_rows(row_of, before, after, r, store):
        for j in range(HALO):
            row = row_of(j)
            low = pltpu.roll(before, (r - STRIP * (j + 1) + LANES) % LANES, 1)
            high = pltpu.roll(after, (2 * LANES - r - STRIP * j) % LANES, 1)
            store(j, 0, jnp.where(lane < r, low, pltpu.roll(row, r, 1)))
            store(j, 1, jnp.where(lane >= LANES - r, high, pltpu.roll(row, LANES - r, 1)))

    def shift(rnd, q, rates):
        for slot in range(2):
            field = 2 * rnd + slot

            def store(j, k, value):
                side[field, k, HALO + q * HALO + j] = value

            shift_rows(lambda j: row_of(field, q * HALO + j), got_i[rnd, 0, q, slot],
                       got_i[rnd, 1, q, slot], rates[slot], store)

    def shift_halo(rnd, rates):
        for slot in range(2):
            field = 2 * rnd + slot

            def store(j, k, value):
                side[field, k, halo_start + j] = value

            rows = got_d.at[rnd, slot]
            center[field, pl.ds(HALO + halo_start, HALO)] = rows[...]
            shift_rows(lambda j: rows[j], got_c[rnd, 0, slot], got_c[rnd, 1, slot], rates[slot], store)

    def patches(taps, field, r, sign, d):
        blocks = []
        for a, b in taps:
            start = HALO + d + sign * (b - a) * r
            if a:
                rows = [side[field, (sign * a + 1) // 2, start + j] for j in range(STEP)]
            else:
                rows = [center[field, HALO + start + j] for j in range(STEP)]
            blocks.append(jnp.concatenate(rows, axis=1))
        return jnp.concatenate(blocks, axis=0)

    def apply(weight, *which):
        taps = [w_center[weight] if w == 0 else w_side[weight] for w in which]
        return taps[0] if len(taps) == 1 else jnp.concatenate(taps, axis=1)

    loads[1].wait()
    loads[2].wait()
    enter(edge_chunk)
    pack(0, edge_chunk)
    loads[3].wait()
    loads[4].wait()

    def enter_more(n, _):
        enter(order(n))
        pack(0, order(n))
        return 0

    ahead = 3
    lax.fori_loop(0, ahead, enter_more, 0)
    pl.semaphore_wait(barrier, len(peers))
    def strips_out(rnd, q):
        for k in range(2):
            strip_copy(rnd, k, q).start()

    def corners_out(rnd):
        for k in range(2):
            corner_copy(rnd, k).start()

    def first_strips(n, _):
        strips_out(0, order(n))
        return 0

    corners_out(0)
    lax.fori_loop(0, ahead, first_strips, 0)
    strips_out(0, edge_chunk)
    edge_copy(0).start()

    def enter_rest(n, _):
        enter_more(n, 0)
        strips_out(0, order(n))
        return 0

    lax.fori_loop(ahead, CHUNKS - 1, enter_rest, 0)
    edge_copy(1).start()

    for copy in loads[5:]:
        copy.wait()
    bias[...] = jnp.broadcast_to(jnp.transpose(jnp.broadcast_to(b1[...], (C, C)))[:, :1], (C, LANES))
    for k, ref in enumerate((w1, w2)):
        taps = [ref[t] for t in range(9)]
        turned = [jnp.transpose(t.astype(F32)).astype(BF16) for t in taps]
        for m, blocks in ((2 * k, taps), (2 * k + 1, turned)):
            w_side[m] = jnp.concatenate(blocks[:3] + blocks[6:], axis=1)
            w_center[m] = jnp.concatenate(blocks[3:6], axis=1)

    def middle_center(q):
        for step in range(HALO // STEP):
            d = q * HALO + step * STEP
            pre = jnp.dot(w_center[0], patches(CENTER, 0, r1, 1, d), preferred_element_type=F32)
            back = jnp.dot(w_center[3], patches(CENTER, 1, r2, -1, d), preferred_element_type=F32)
            for j in range(STEP):
                conv[d + j] = pre[:, j * LANES : (j + 1) * LANES] + bias[...]
                conv_back[d + j] = back[:, j * LANES : (j + 1) * LANES]

    def middle(d):
        pre = jnp.dot(w_side[0], patches(SIDE, 0, r1, 1, d), preferred_element_type=F32)
        back = jnp.dot(w_side[3], patches(SIDE, 1, r2, -1, d), preferred_element_type=F32)
        for j in range(STEP):
            m = maskf[pl.ds(d + j, 1), :]
            y = pre[:, j * LANES : (j + 1) * LANES] + conv[d + j]
            s = sigmoid(y)
            center[2, PAD + d + j] = (y * s * m).astype(BF16)
            grad = back[:, j * LANES : (j + 1) * LANES] + conv_back[d + j]
            center[3, PAD + d + j] = (grad * m * (s * (1.0 + y * (1.0 - s)))).astype(BF16)

    def center_step(n, _):
        middle_center(order(n))
        return 0

    lax.fori_loop(0, CHUNKS - 1, center_step, 0)

    def middle_chunk(q):
        for step in range(HALO // STEP):
            middle(q * HALO + step * STEP)

    settle(0, order(0))
    shift(0, order(0), (r1, r2))

    def middle_step(n, _):
        settle(0, order(n + 1))
        shift(0, order(n + 1), (r1, r2))
        middle_chunk(order(n))
        return 0

    lax.fori_loop(0, CHUNKS - 1, middle_step, 0)
    settle_halo(0)
    shift_halo(0, (r1, r2))
    middle_center(edge_chunk)
    middle_chunk(edge_chunk)
    edge_copy(2).start()

    wide = 32
    nt = (((1,), (1,)), ((), ()))

    def row_block(rows):
        return jnp.concatenate(rows, axis=1)

    def near_rows(field, k):
        before = row_block([side[field, 0, k + j] for j in range(wide)])
        same = row_block([center[field, HALO + k + j] for j in range(wide)])
        return [before, same, row_block([side[field, 1, k + j] for j in range(wide)])]

    def grads(n, carry):
        k = n * wide
        act = near_rows(0, k)
        act.append(jnp.ones((C, wide * LANES), BF16))
        ups = [row_block([center[3, HALO + k - m * r1 + j] for j in range(wide)]) for m in LAGS]
        one = lax.dot_general(jnp.concatenate(ups, axis=0), jnp.concatenate(act, axis=0), nt,
                              preferred_element_type=F32)
        grad = near_rows(1, k)
        hid = [row_block([center[2, HALO + k + m * r2 + j] for j in range(wide)]) for m in LAGS]
        two = lax.dot_general(jnp.concatenate(grad, axis=0), jnp.concatenate(hid, axis=0), nt,
                              preferred_element_type=F32)
        return carry[0] + one, carry[1] + two

    zero = (jnp.zeros((5 * C, 4 * C), F32), jnp.zeros((3 * C, 5 * C), F32))
    one, two = lax.fori_loop(0, EXT // wide, grads, zero, unroll=2)

    def block(value, i, j):
        return value[C * i : C * (i + 1), C * j : C * (j + 1)]

    blocks = [[block(one, b - a + 2, a + 1) for a, b in TAPS], [block(two, 1 - a, b - a + 2) for a, b in TAPS]]
    rows = [jnp.concatenate(blocks[k][4 * p : 4 * p + 4], axis=1) for k in range(2) for p in range(2)]
    rows.append(jnp.concatenate([blocks[0][8], blocks[1][8], block(one, 2, 3), jnp.zeros((C, C), F32)], axis=1))
    rows = jnp.concatenate(rows, axis=0)
    for k in range(GROUP):
        sums[k] = rows[PART_ROWS * k : PART_ROWS * (k + 1)]

    def scatter(step):
        rank, device = near_peer(step)
        return rank, pltpu.make_async_remote_copy(
            src_ref=sums.at[rank], dst_ref=got.at[step], send_sem=send1.at[step],
            recv_sem=recv1.at[step], device_id=device, device_id_type=MESH)

    for step in ORDER:
        scatter(step)[1].start()
    edge_copy(3).start()

    pack(1, edge_chunk)
    strips_out(1, edge_chunk)
    corners_out(1)

    def launch_rest(n, _):
        pack(1, order(n))
        strips_out(1, order(n))
        return 0

    lax.fori_loop(0, CHUNKS - 1, launch_rest, 0)

    spread = []
    for step in ORDER:
        rank, device = far_peer(step)
        spread.append(pltpu.make_async_remote_copy(
            src_ref=part.at[far], dst_ref=part.at[far], send_sem=send2.at[step],
            recv_sem=recv2.at[step], device_id=device, device_id_type=MESH))

    value = sums[near]
    for step in ORDER:
        scatter(step)[1].wait_recv()
        value = value + got[step]
    part[far] = value
    for copy in spread:
        copy.start()

    def last_conv(weight, field, r, sign, q):
        for step in range(HALO // STEP):
            d = q * HALO + step * STEP
            taps = patches(SIDE + CENTER, field, r, sign, d)
            y = jnp.dot(apply(weight, 1, 0), taps, preferred_element_type=F32)
            for j in range(STEP):
                conv[d + j] = y[:, j * LANES : (j + 1) * LANES]

    settle(1, order(0))
    shift(1, order(0), (r2, r1))

    def forward(n, _):
        settle(1, order(n + 1))
        shift(1, order(n + 1), (r2, r1))
        last_conv(2, 2, r2, 1, order(n))
        return 0

    lax.fori_loop(0, CHUNKS - 1, forward, 0)
    settle_halo(1)
    shift_halo(1, (r2, r1))
    last_conv(2, 2, r2, 1, edge_chunk)

    def finish_forward(q, _):
        rows = pl.ds(pl.multiple_of(q * HALO, HALO), HALO)
        y = jnp.transpose(conv[rows], (1, 0, 2))
        out[:, rows, :] = (feat[:, rows, :].astype(F32) + maskf[rows, :][None] * y).astype(BF16)
        return 0

    lax.fori_loop(0, CHUNKS, finish_forward, 0)
    store_out = pltpu.make_async_copy(out, out_hbm, load.at[0])
    store_out.start()
    def gather(step):
        return near_peer(step)[0], pltpu.make_async_remote_copy(
            src_ref=total.at[near], dst_ref=total.at[near], send_sem=send3.at[step],
            recv_sem=recv3.at[step], device_id=near_peer(step)[1], device_id_type=MESH)

    for copy in spread:
        copy.wait_recv()
    value = part[0]
    for rank in range(1, GROUP):
        value = value + part[rank]
    total[near] = value
    for step in ORDER:
        gather(step)[1].start()

    def backward(q, _):
        last_conv(1, 3, r1, -1, q)
        return 0

    lax.fori_loop(0, CHUNKS, backward, 0)

    def finish_backward(q, _):
        rows = pl.ds(pl.multiple_of(q * HALO, HALO), HALO)
        y = jnp.transpose(conv[rows], (1, 0, 2))
        x = feat[:, rows, :].astype(F32)
        s = sigmoid(x)
        slope = maskf[rows, :][None] * (s * (1.0 + x * (1.0 - s)))
        gfeat[:, rows, :] = (cot[:, rows, :].astype(F32) + slope * y).astype(BF16)
        return 0

    lax.fori_loop(0, CHUNKS, finish_backward, 0)
    store_gfeat = pltpu.make_async_copy(gfeat, gfeat_hbm, load.at[1])
    store_gfeat.start()
    for field in range(4):
        edge_copy(field).wait_send()

    def sent(q, _):
        for rnd in range(2):
            for side in range(2):
                strip_copy(rnd, side, q).wait_send()
        return 0

    lax.fori_loop(0, CHUNKS, sent, 0)
    for rnd in range(2):
        for side in range(2):
            corner_copy(rnd, side).wait_send()
    for step in ORDER:
        scatter(step)[1].wait_send()
    for copy in spread:
        copy.wait_send()
    for step in ORDER:
        gather(step)[1].wait()

    factor = 1.0 / jnp.sqrt(jnp.float32(CELLS))
    rows = jnp.concatenate([total[k] for k in range(GROUP)], axis=0) * factor
    last = rows[4 * C :]
    for k, ref in enumerate((g1, g2)):
        for t in range(8):
            base = C * (2 * k + t // 4)
            ref[t] = rows[base : base + C, C * (t % 4) : C * (t % 4 + 1)]
        ref[8] = last[:, C * k : C * (k + 1)]
    gb[...] = jnp.transpose(last[:, 2 * C : 3 * C])[:1]
    store_out.wait()
    store_gfeat.wait()


def hand_over(*refs):
    given, results, held, sems = refs[:5], refs[5:10], refs[10:15], refs[15]
    loads = [pltpu.make_async_copy(given[k], held[k], sems.at[k]) for k in range(5)]
    stores = [pltpu.make_async_copy(held[k], results[k], sems.at[5 + k]) for k in range(5)]
    for copy in loads:
        copy.start()
    for load, store in zip(loads, stores):
        load.wait()
        store.start()
    for copy in stores:
        copy.wait()


def shards(features, cotangent, band_mask, dilation, w_first, b_first, w_second):
    vmem = pl.BlockSpec(memory_space=pltpu.VMEM)
    dma = pltpu.SemaphoreType.DMA
    shape = jax.ShapeDtypeStruct
    field = (C, ROWS, LANES)
    taps = (9, C, C)
    hbm = pl.BlockSpec(memory_space=pltpu.HBM)
    results = pl.pallas_call(
        kernel,
        out_shape=[shape(field, BF16), shape(field, BF16), shape(taps, F32), shape((1, C), F32), shape(taps, F32)],
        in_specs=[pl.BlockSpec(memory_space=pltpu.SMEM)] + [hbm] * 6,
        out_specs=[hbm] * 2 + [vmem] * 3,
        scratch_shapes=[
            pltpu.VMEM(field, BF16),
            pltpu.VMEM(field, BF16),
            pltpu.VMEM(field, BF16),
            pltpu.VMEM(field, BF16),
            pltpu.VMEM((ROWS, LANES), jnp.int32),
            pltpu.VMEM(taps, BF16),
            pltpu.VMEM((1, C), F32),
            pltpu.VMEM(taps, BF16),
            pltpu.VMEM((4, ROWS + 2 * PAD, C, LANES), BF16),
            pltpu.VMEM((2, 2, CHUNKS, 2, C, LANES), BF16),
            pltpu.VMEM((4, 2, EXT, C, LANES), BF16),
            pltpu.VMEM((ROWS, LANES), F32),
            pltpu.VMEM((4, C, 6 * C), BF16),
            pltpu.VMEM((4, C, 3 * C), BF16),
            pltpu.VMEM((C, LANES), F32),
            pltpu.VMEM((ROWS, C, LANES), F32),
            pltpu.VMEM((ROWS, C, LANES), F32),
            pltpu.VMEM((2, 2, HALO, C, LANES), BF16),
            pltpu.VMEM((2, 2, CHUNKS, 2, C, LANES), BF16),
            pltpu.VMEM((2, 2, 2, C, LANES), BF16),
            pltpu.VMEM((GROUP, PART_ROWS, LANES), F32),
            pltpu.VMEM((GROUP, PART_ROWS, LANES), F32),
            pltpu.VMEM((GROUP, PART_ROWS, LANES), F32),
            pltpu.VMEM((GROUP, PART_ROWS, LANES), F32),
            dma((8,)),
            dma((2, 2)), dma((2, 2)), dma((2, 2, CHUNKS)), dma((2, 2, CHUNKS)), dma((2, 2)), dma((2, 2)),
            dma((GROUP,)), dma((GROUP,)), dma((GROUP,)), dma((GROUP,)), dma((GROUP,)), dma((GROUP,)),
        ],
        compiler_params=pltpu.CompilerParams(
            collective_id=0, has_side_effects=True, vmem_limit_bytes=63 * 1024 * 1024
        ),
    )(dilation, features, cotangent, band_mask, jnp.transpose(w_first, (1, 0, 2)), b_first[None],
      jnp.transpose(w_second, (1, 0, 2)))
    out, gfeat, g1, gb, g2 = pl.pallas_call(
        hand_over,
        out_shape=[shape(r.shape, r.dtype) for r in results],
        in_specs=[hbm] * 5,
        out_specs=[hbm] * 5,
        scratch_shapes=[pltpu.VMEM(r.shape, r.dtype) for r in results] + [dma((10,))],
        compiler_params=pltpu.CompilerParams(vmem_limit_bytes=63 * 1024 * 1024),
    )(*results)
    return (out, gfeat, jnp.transpose(g1, (1, 0, 2)), gb[0], jnp.transpose(g2, (1, 0, 2)))


def solution(mesh):
    field, whole = P(None, "diag", "bins"), P()
    return jax.shard_map(
        shards, mesh=mesh, in_specs=(field, field, P("diag", "bins"), whole, whole, whole, whole),
        out_specs=(field, field, whole, whole, whole), check_vma=False)
```

time: 54.6 us -> 46.8 us (0.86)
  the two profiles are of different devices: /device:TPU:4 before, /device:TPU:1 now
where the time goes in v3:
time: 46.8 us; the launch traced here: 46.1 us
  Pallas kernels  45.5 us (97%)
  between operations  0.64 us (1%)
    pallas_call x1, Pallas kernels, shards(): pl.pallas_call(kernel, out_shape=[shape(field, BF16), shape(field, BF16),...  43 us
    pallas_call x1, Pallas kernels, shards(): pl.pallas_call(hand_over, out_shape=[shape(r.shape, r.dtype) for r in res...  2.45 us

profile of v3, /device:TPU:1, one launch (start us, length us, event | category | flops | bytes accessed | tf_op | source)
XLA Modules:
  0.0 46.1 jit_solution(11459451912008843393)
XLA Ops:
  0.6 43.0 %shard_map.110 = (bf16[32,96,128]{2,1,0:T(8,128)(2,1)}, bf16[32,96,128]{2,1,0:T(8,128)(2,1)}, f32[9,32,32]{2,1,0:T(8,128)}, f32[1,32]{1,0:T(1,128)}, f32[9,32,32]{2,1,0:T(8,128)}) custom-call(s32[2]{0:T(128)} %rate.1, bf16[32,96,128]{2,1,0:T(8,128)(2,1)} %feat_in.1, bf16[32,96,128]{2,1,0:T(8,128)(2,1)} %cot_in.1, s32[96,128]{1,0:T(8,128)} %mask_in.1, ...), custom_call_target="tpu_custom_call" | custom-call | tf_op jit(solution)/shard_map/pallas_call | solution.py:486
  43.6 2.5 %shard_map.111 = (bf16[32,96,128]{2,1,0:T(8,128)(2,1)}, bf16[32,96,128]{2,1,0:T(8,128)(2,1)}, f32[9,32,32]{2,1,0:T(8,128)}, f32[1,32]{1,0:T(1,128)}, f32[9,32,32]{2,1,0:T(8,128)}) custom-call(bf16[32,96,128]{2,1,0:T(8,128)(2,1)} %get-tuple-element.15.refs_0_, bf16[32,96,128]{2,1,0:T(8,128)(2,1)} %get-tuple-element.16.refs_1_, ...), custom_call_target="tpu_custom_call" | custom-call | tf_op jit(solution)/shard_map/pallas_call | solution.py:525

commit v4 on v3

--- a/solution.py
+++ b/solution.py
@@ -33,8 +33,8 @@
 
 def kernel(
     rate, feat_in, cot_in, mask_in, w1_in, b1_in, w2_in,
-    out_hbm, gfeat_hbm, g1, gb, g2,
-    out, gfeat, feat, cot, mask, w1, b1, w2, center, strips, side, maskf, w_side, w_center, bias, conv, conv_back,
+    out, gfeat, g1, gb, g2,
+    feat, cot, mask, w1, b1, w2, center, strips, side, maskf, w_side, w_center, bias, conv, conv_back,
     got_d, got_i, got_c, sums, got, part, total, load,
     send_d, recv_d, send_i, recv_i, send_c, recv_c, send1, recv1, send2, recv2, send3, recv3,
 ):
@@ -396,8 +396,6 @@
         return 0
 
     lax.fori_loop(0, CHUNKS, finish_forward, 0)
-    store_out = pltpu.make_async_copy(out, out_hbm, load.at[0])
-    store_out.start()
     def gather(step):
         return near_peer(step)[0], pltpu.make_async_remote_copy(
             src_ref=total.at[near], dst_ref=total.at[near], send_sem=send3.at[step],
@@ -428,8 +426,6 @@
         return 0
 
     lax.fori_loop(0, CHUNKS, finish_backward, 0)
-    store_gfeat = pltpu.make_async_copy(gfeat, gfeat_hbm, load.at[1])
-    store_gfeat.start()
     for field in range(4):
         edge_copy(field).wait_send()
 
@@ -459,20 +455,14 @@
             ref[t] = rows[base : base + C, C * (t % 4) : C * (t % 4 + 1)]
         ref[8] = last[:, C * k : C * (k + 1)]
     gb[...] = jnp.transpose(last[:, 2 * C : 3 * C])[:1]
-    store_out.wait()
-    store_gfeat.wait()
 
 
 def hand_over(*refs):
-    given, results, held, sems = refs[:5], refs[5:10], refs[10:15], refs[15]
-    loads = [pltpu.make_async_copy(given[k], held[k], sems.at[k]) for k in range(5)]
-    stores = [pltpu.make_async_copy(held[k], results[k], sems.at[5 + k]) for k in range(5)]
-    for copy in loads:
+    given, results, sems = refs[:5], refs[5:10], refs[10]
+    copies = [pltpu.make_async_copy(given[k], results[k], sems.at[k]) for k in range(5)]
+    for copy in copies:
         copy.start()
-    for load, store in zip(loads, stores):
-        load.wait()
-        store.start()
-    for copy in stores:
+    for copy in copies:
         copy.wait()
 
 
@@ -485,12 +475,10 @@
     hbm = pl.BlockSpec(memory_space=pltpu.HBM)
     results = pl.pallas_call(
         kernel,
-        out_shape=[shape(field, BF16), shape(field, BF16), shape(taps, F32), shape((1, C), F32), shape(taps, F32)],
+        out_shape=[pltpu.VMEM(field, BF16), pltpu.VMEM(field, BF16), pltpu.VMEM(taps, F32), pltpu.VMEM((1, C), F32), pltpu.VMEM(taps, F32)],
         in_specs=[pl.BlockSpec(memory_space=pltpu.SMEM)] + [hbm] * 6,
-        out_specs=[hbm] * 2 + [vmem] * 3,
+        out_specs=[vmem] * 5,
         scratch_shapes=[
-            pltpu.VMEM(field, BF16),
-            pltpu.VMEM(field, BF16),
             pltpu.VMEM(field, BF16),
             pltpu.VMEM(field, BF16),
             pltpu.VMEM((ROWS, LANES), jnp.int32),
@@ -518,17 +506,17 @@
             dma((GROUP,)), dma((GROUP,)), dma((GROUP,)), dma((GROUP,)), dma((GROUP,)), dma((GROUP,)),
         ],
         compiler_params=pltpu.CompilerParams(
-            collective_id=0, has_side_effects=True, vmem_limit_bytes=63 * 1024 * 1024
+            collective_id=0, has_side_effects=True, vmem_limit_bytes=61 * 1024 * 1024
         ),
     )(dilation, features, cotangent, band_mask, jnp.transpose(w_first, (1, 0, 2)), b_first[None],
       jnp.transpose(w_second, (1, 0, 2)))
     out, gfeat, g1, gb, g2 = pl.pallas_call(
         hand_over,
         out_shape=[shape(r.shape, r.dtype) for r in results],
-        in_specs=[hbm] * 5,
+        in_specs=[vmem] * 5,
         out_specs=[hbm] * 5,
-        scratch_shapes=[pltpu.VMEM(r.shape, r.dtype) for r in results] + [dma((10,))],
-        compiler_params=pltpu.CompilerParams(vmem_limit_bytes=63 * 1024 * 1024),
+        scratch_shapes=[dma((5,))],
+        compiler_params=pltpu.CompilerParams(vmem_limit_bytes=8 * 1024 * 1024),
     )(*results)
     return (out, gfeat, jnp.transpose(g1, (1, 0, 2)), gb[0], jnp.transpose(g2, (1, 0, 2)))
 

time: 46.8 us -> 44.4 us (0.949); the launches traced: 46.1 us -> 44.2 us
  Pallas kernels: 45.5 us -> 43.6 us
    pallas_call x1, Pallas kernels: 2.45 us -> 1.28 us  [shards(): pl.pallas_call(hand_over, out_shape=[shape(r.shape, r.dtype) for r in res...]
    pallas_call x1, Pallas kernels: 43 us -> 42.3 us  [shards(): pl.pallas_call(kernel, out_shape=[pltpu.VMEM(field, BF16), pltpu.VMEM(fie...]
where the time goes in v4:
time: 44.4 us; the launch traced here: 44.2 us
  Pallas kernels  43.6 us (98%)
  between operations  0.64 us (1%)
    pallas_call x1, Pallas kernels, shards(): pl.pallas_call(kernel, out_shape=[pltpu.VMEM(field, BF16), pltpu.VMEM(fie...  42.3 us
    pallas_call x1, Pallas kernels, shards(): pl.pallas_call(hand_over, out_shape=[shape(r.shape, r.dtype) for r in res...  1.28 us

profile of v4, /device:TPU:1, one launch (start us, length us, event | category | flops | bytes accessed | tf_op | source)
XLA Modules:
  0.0 44.2 jit_solution(12505544332870105378)
XLA Ops:
  0.6 42.3 %shard_map.110 = (bf16[32,96,128]{2,1,0:T(8,128)(2,1)S(1)}, bf16[32,96,128]{2,1,0:T(8,128)(2,1)S(1)}, f32[9,32,32]{2,1,0:T(8,128)S(1)}, f32[1,32]{1,0:T(1,128)S(1)}, f32[9,32,32]{2,1,0:T(8,128)S(1)}) custom-call(s32[2]{0:T(128)} %rate.1, bf16[32,96,128]{2,1,0:T(8,128)(2,1)} %feat_in.1, bf16[32,96,128]{2,1,0:T(8,128)(2,1)} %cot_in.1, s32[96,128]{1,0:T(8,128)} %mask_in.1, ...), custom_call_target="tpu_custom_call" | custom-call | tf_op jit(solution)/shard_map/pallas_call | solution.py:476
  42.9 1.3 %shard_map.111 = (bf16[32,96,128]{2,1,0:T(8,128)(2,1)}, bf16[32,96,128]{2,1,0:T(8,128)(2,1)}, f32[9,32,32]{2,1,0:T(8,128)}, f32[1,32]{1,0:T(1,128)}, f32[9,32,32]{2,1,0:T(8,128)}) custom-call(bf16[32,96,128]{2,1,0:T(8,128)(2,1)S(1)} %get-tuple-element.15.refs_0_, bf16[32,96,128]{2,1,0:T(8,128)(2,1)S(1)} %get-tuple-element.16.refs_1_, ...), custom_call_target="tpu_custom_call" | custom-call | tf_op jit(solution)/shard_map/pallas_call | solution.py:513

commit v5 on v4

--- a/solution.py
+++ b/solution.py
@@ -34,10 +34,11 @@
 def kernel(
     rate, feat_in, cot_in, mask_in, w1_in, b1_in, w2_in,
     out, gfeat, g1, gb, g2,
-    feat, cot, mask, w1, b1, w2, center, strips, side, maskf, w_side, w_center, bias, conv, conv_back,
+    feat, cot, mask, w1, b1, w2, c0, c1, c2, c3, strips, s0, s1, s2, s3, s4, s5, s6, s7, maskf, w_side, w_center, bias, conv, conv_back,
     got_d, got_i, got_c, sums, got, part, total, load,
     send_d, recv_d, send_i, recv_i, send_c, recv_c, send1, recv1, send2, recv2, send3, recv3,
 ):
+    center, side = (c0, c1, c2, c3), ((s0, s1), (s2, s3), (s4, s5), (s6, s7))
     bins, diag = lax.axis_index("bins"), lax.axis_index("diag")
     count = lax.axis_size("bins")
     right, left = (bins + 1) % count, (bins + count - 1) % count
@@ -83,10 +84,10 @@
     for copy in loads:
         copy.start()
     for field in range(4):
-        center[field, :PAD] = jnp.zeros((PAD, C, LANES), BF16)
-        center[field, PAD + ROWS :] = jnp.zeros((PAD, C, LANES), BF16)
+        center[field][:PAD] = jnp.zeros((PAD, C, LANES), BF16)
+        center[field][PAD + ROWS :] = jnp.zeros((PAD, C, LANES), BF16)
         for k in range(2):
-            side[field, k, pl.ds(zero_start, HALO)] = jnp.zeros((HALO, C, LANES), BF16)
+            side[field][k][pl.ds(zero_start, HALO)] = jnp.zeros((HALO, C, LANES), BF16)
     loads[0].wait()
     maskf[...] = mask[...].astype(F32)
 
@@ -95,12 +96,12 @@
         m = maskf[rows, :][None]
         x = feat[:, rows, :].astype(F32)
         inner = pl.ds(pl.multiple_of(PAD + q * HALO, HALO), HALO)
-        center[0, inner] = jnp.transpose((x * sigmoid(x) * m).astype(BF16), (1, 0, 2))
+        center[0][inner] = jnp.transpose((x * sigmoid(x) * m).astype(BF16), (1, 0, 2))
         grad = (cot[:, rows, :].astype(F32) * m).astype(BF16)
-        center[1, inner] = jnp.transpose(grad, (1, 0, 2))
+        center[1][inner] = jnp.transpose(grad, (1, 0, 2))
 
     def row_of(field, d):
-        return center[field, PAD + d]
+        return center[field][PAD + d]
 
     def strip_copy(rnd, side, q):
         return pltpu.make_async_remote_copy(
@@ -132,7 +133,7 @@
     def edge_copy(field):
         rnd, slot = field // 2, field % 2
         return pltpu.make_async_remote_copy(
-            src_ref=center.at[field, pl.ds(PAD + edge_start, HALO)], dst_ref=got_d.at[rnd, slot],
+            src_ref=center[field].at[pl.ds(PAD + edge_start, HALO)], dst_ref=got_d.at[rnd, slot],
             send_sem=send_d.at[rnd, slot], recv_sem=recv_d.at[rnd, slot],
             device_id=(bins, across), device_id_type=MESH)
 
@@ -154,43 +155,44 @@
             def _():
                 got_c[rnd, side] = jnp.zeros((2, C, LANES), BF16)
 
-    def shift_rows(row_of, before, after, r, store):
-        for j in range(HALO):
+    def shift_rows(row_of, before, after, r, store, which):
+        for j in which:
             row = row_of(j)
             low = pltpu.roll(before, (r - STRIP * (j + 1) + LANES) % LANES, 1)
             high = pltpu.roll(after, (2 * LANES - r - STRIP * j) % LANES, 1)
             store(j, 0, jnp.where(lane < r, low, pltpu.roll(row, r, 1)))
             store(j, 1, jnp.where(lane >= LANES - r, high, pltpu.roll(row, LANES - r, 1)))
 
-    def shift(rnd, q, rates):
+    def shift(rnd, q, rates, which=range(HALO)):
         for slot in range(2):
             field = 2 * rnd + slot
 
             def store(j, k, value):
-                side[field, k, HALO + q * HALO + j] = value
+                side[field][k][HALO + q * HALO + j] = value
 
             shift_rows(lambda j: row_of(field, q * HALO + j), got_i[rnd, 0, q, slot],
-                       got_i[rnd, 1, q, slot], rates[slot], store)
-
-    def shift_halo(rnd, rates):
+                       got_i[rnd, 1, q, slot], rates[slot], store, which)
+
+    def shift_halo(rnd, rates, which=range(HALO)):
         for slot in range(2):
             field = 2 * rnd + slot
 
             def store(j, k, value):
-                side[field, k, halo_start + j] = value
+                side[field][k][halo_start + j] = value
 
             rows = got_d.at[rnd, slot]
-            center[field, pl.ds(HALO + halo_start, HALO)] = rows[...]
-            shift_rows(lambda j: rows[j], got_c[rnd, 0, slot], got_c[rnd, 1, slot], rates[slot], store)
+            for j in which:
+                center[field][HALO + halo_start + j] = rows[j]
+            shift_rows(lambda j: rows[j], got_c[rnd, 0, slot], got_c[rnd, 1, slot], rates[slot], store, which)
 
     def patches(taps, field, r, sign, d):
         blocks = []
         for a, b in taps:
             start = HALO + d + sign * (b - a) * r
             if a:
-                rows = [side[field, (sign * a + 1) // 2, start + j] for j in range(STEP)]
+                rows = [side[field][(sign * a + 1) // 2][start + j] for j in range(STEP)]
             else:
-                rows = [center[field, HALO + start + j] for j in range(STEP)]
+                rows = [center[field][HALO + start + j] for j in range(STEP)]
             blocks.append(jnp.concatenate(rows, axis=1))
         return jnp.concatenate(blocks, axis=0)
 
@@ -264,9 +266,9 @@
             m = maskf[pl.ds(d + j, 1), :]
             y = pre[:, j * LANES : (j + 1) * LANES] + conv[d + j]
             s = sigmoid(y)
-            center[2, PAD + d + j] = (y * s * m).astype(BF16)
+            center[2][PAD + d + j] = (y * s * m).astype(BF16)
             grad = back[:, j * LANES : (j + 1) * LANES] + conv_back[d + j]
-            center[3, PAD + d + j] = (grad * m * (s * (1.0 + y * (1.0 - s)))).astype(BF16)
+            center[3][PAD + d + j] = (grad * m * (s * (1.0 + y * (1.0 - s)))).astype(BF16)
 
     def center_step(n, _):
         middle_center(order(n))
@@ -274,52 +276,54 @@
 
     lax.fori_loop(0, CHUNKS - 1, center_step, 0)
 
-    def middle_chunk(q):
+    def middle_chunk(q, beside=None):
         for step in range(HALO // STEP):
             middle(q * HALO + step * STEP)
-
-    settle(0, order(0))
-    shift(0, order(0), (r1, r2))
+            if beside is not None:
+                beside(range(step * STEP, step * STEP + STEP))
+
+    for n in range(2):
+        settle(0, order(n))
+        shift(0, order(n), (r1, r2))
 
     def middle_step(n, _):
-        settle(0, order(n + 1))
-        shift(0, order(n + 1), (r1, r2))
-        middle_chunk(order(n))
-        return 0
-
-    lax.fori_loop(0, CHUNKS - 1, middle_step, 0)
+        settle(0, order(n + 2))
+        middle_chunk(order(n), lambda which: shift(0, order(n + 2), (r1, r2), which))
+        return 0
+
+    lax.fori_loop(0, CHUNKS - 2, middle_step, 0)
     settle_halo(0)
-    shift_halo(0, (r1, r2))
+    middle_chunk(order(CHUNKS - 2), lambda which: shift_halo(0, (r1, r2), which))
     middle_center(edge_chunk)
     middle_chunk(edge_chunk)
     edge_copy(2).start()
 
-    wide = 32
+    wide = 28
     nt = (((1,), (1,)), ((), ()))
 
     def row_block(rows):
         return jnp.concatenate(rows, axis=1)
 
     def near_rows(field, k):
-        before = row_block([side[field, 0, k + j] for j in range(wide)])
-        same = row_block([center[field, HALO + k + j] for j in range(wide)])
-        return [before, same, row_block([side[field, 1, k + j] for j in range(wide)])]
+        before = row_block([side[field][0][k + j] for j in range(wide)])
+        same = row_block([center[field][HALO + k + j] for j in range(wide)])
+        return [before, same, row_block([side[field][1][k + j] for j in range(wide)])]
 
     def grads(n, carry):
-        k = n * wide
+        k = n * wide + HALO * (1 - diag)
         act = near_rows(0, k)
         act.append(jnp.ones((C, wide * LANES), BF16))
-        ups = [row_block([center[3, HALO + k - m * r1 + j] for j in range(wide)]) for m in LAGS]
+        ups = [row_block([center[3][HALO + k - m * r1 + j] for j in range(wide)]) for m in LAGS]
         one = lax.dot_general(jnp.concatenate(ups, axis=0), jnp.concatenate(act, axis=0), nt,
                               preferred_element_type=F32)
         grad = near_rows(1, k)
-        hid = [row_block([center[2, HALO + k + m * r2 + j] for j in range(wide)]) for m in LAGS]
+        hid = [row_block([center[2][HALO + k + m * r2 + j] for j in range(wide)]) for m in LAGS]
         two = lax.dot_general(jnp.concatenate(grad, axis=0), jnp.concatenate(hid, axis=0), nt,
                               preferred_element_type=F32)
         return carry[0] + one, carry[1] + two
 
     zero = (jnp.zeros((5 * C, 4 * C), F32), jnp.zeros((3 * C, 5 * C), F32))
-    one, two = lax.fori_loop(0, EXT // wide, grads, zero, unroll=2)
+    one, two = lax.fori_loop(0, (EXT - HALO) // wide, grads, zero, unroll=2)
 
     def block(value, i, j):
         return value[C * i : C * (i + 1), C * j : C * (j + 1)]
@@ -367,26 +371,28 @@
     for copy in spread:
         copy.start()
 
-    def last_conv(weight, field, r, sign, q):
+    def last_conv(weight, field, r, sign, q, beside=None):
         for step in range(HALO // STEP):
             d = q * HALO + step * STEP
             taps = patches(SIDE + CENTER, field, r, sign, d)
             y = jnp.dot(apply(weight, 1, 0), taps, preferred_element_type=F32)
             for j in range(STEP):
                 conv[d + j] = y[:, j * LANES : (j + 1) * LANES]
-
-    settle(1, order(0))
-    shift(1, order(0), (r2, r1))
+            if beside is not None:
+                beside(range(step * STEP, step * STEP + STEP))
+
+    for n in range(2):
+        settle(1, order(n))
+        shift(1, order(n), (r2, r1))
 
     def forward(n, _):
-        settle(1, order(n + 1))
-        shift(1, order(n + 1), (r2, r1))
-        last_conv(2, 2, r2, 1, order(n))
-        return 0
-
-    lax.fori_loop(0, CHUNKS - 1, forward, 0)
+        settle(1, order(n + 2))
+        last_conv(2, 2, r2, 1, order(n), lambda which: shift(1, order(n + 2), (r2, r1), which))
+        return 0
+
+    lax.fori_loop(0, CHUNKS - 2, forward, 0)
     settle_halo(1)
-    shift_halo(1, (r2, r1))
+    last_conv(2, 2, r2, 1, order(CHUNKS - 2), lambda which: shift_halo(1, (r2, r1), which))
     last_conv(2, 2, r2, 1, edge_chunk)
 
     def finish_forward(q, _):
@@ -437,8 +443,8 @@
 
     lax.fori_loop(0, CHUNKS, sent, 0)
     for rnd in range(2):
-        for side in range(2):
-            corner_copy(rnd, side).wait_send()
+        for way in range(2):
+            corner_copy(rnd, way).wait_send()
     for step in ORDER:
         scatter(step)[1].wait_send()
     for copy in spread:
@@ -485,9 +491,19 @@
             pltpu.VMEM(taps, BF16),
             pltpu.VMEM((1, C), F32),
             pltpu.VMEM(taps, BF16),
-            pltpu.VMEM((4, ROWS + 2 * PAD, C, LANES), BF16),
+            pltpu.VMEM((ROWS + 2 * PAD, C, LANES), BF16),
+            pltpu.VMEM((ROWS + 2 * PAD, C, LANES), BF16),
+            pltpu.VMEM((ROWS + 2 * PAD, C, LANES), BF16),
+            pltpu.VMEM((ROWS + 2 * PAD, C, LANES), BF16),
             pltpu.VMEM((2, 2, CHUNKS, 2, C, LANES), BF16),
-            pltpu.VMEM((4, 2, EXT, C, LANES), BF16),
+            pltpu.VMEM((EXT, C, LANES), BF16),
+            pltpu.VMEM((EXT, C, LANES), BF16),
+            pltpu.VMEM((EXT, C, LANES), BF16),
+            pltpu.VMEM((EXT, C, LANES), BF16),
+            pltpu.VMEM((EXT, C, LANES), BF16),
+            pltpu.VMEM((EXT, C, LANES), BF16),
+            pltpu.VMEM((EXT, C, LANES), BF16),
+            pltpu.VMEM((EXT, C, LANES), BF16),
             pltpu.VMEM((ROWS, LANES), F32),
             pltpu.VMEM((4, C, 6 * C), BF16),
             pltpu.VMEM((4, C, 3 * C), BF16),

time: 44.4 us -> 42.5 us (0.957)
  Pallas kernels: 43.6 us -> 41.7 us
    pallas_call x1, Pallas kernels: 42.3 us -> 40.4 us  [shards(): pl.pallas_call(kernel, out_shape=[pltpu.VMEM(field, BF16), pltpu.VMEM(fie...]
where the time goes in v5:
time: 42.5 us; the launch traced here: 42.3 us
  Pallas kernels  41.7 us (98%)
  between operations  0.64 us (2%)
    pallas_call x1, Pallas kernels, shards(): pl.pallas_call(kernel, out_shape=[pltpu.VMEM(field, BF16), pltpu.VMEM(fie...  40.4 us
    pallas_call x1, Pallas kernels, shards(): pl.pallas_call(hand_over, out_shape=[shape(r.shape, r.dtype) for r in res...  1.28 us

profile of v5, /device:TPU:1, one launch (start us, length us, event | category | flops | bytes accessed | tf_op | source)
XLA Modules:
  0.0 42.3 jit_solution(3964453572904640530)
XLA Ops:
  0.6 40.4 %shard_map.110 = (bf16[32,96,128]{2,1,0:T(8,128)(2,1)S(1)}, bf16[32,96,128]{2,1,0:T(8,128)(2,1)S(1)}, f32[9,32,32]{2,1,0:T(8,128)S(1)}, f32[1,32]{1,0:T(1,128)S(1)}, f32[9,32,32]{2,1,0:T(8,128)S(1)}) custom-call(s32[2]{0:T(128)} %rate.1, bf16[32,96,128]{2,1,0:T(8,128)(2,1)} %feat_in.1, bf16[32,96,128]{2,1,0:T(8,128)(2,1)} %cot_in.1, s32[96,128]{1,0:T(8,128)} %mask_in.1, ...), custom_call_target="tpu_custom_call" | custom-call | tf_op jit(solution)/shard_map/pallas_call | solution.py:482
  41.1 1.3 %shard_map.111 = (bf16[32,96,128]{2,1,0:T(8,128)(2,1)}, bf16[32,96,128]{2,1,0:T(8,128)(2,1)}, f32[9,32,32]{2,1,0:T(8,128)}, f32[1,32]{1,0:T(1,128)}, f32[9,32,32]{2,1,0:T(8,128)}) custom-call(bf16[32,96,128]{2,1,0:T(8,128)(2,1)S(1)} %get-tuple-element.15.refs_0_, bf16[32,96,128]{2,1,0:T(8,128)(2,1)S(1)} %get-tuple-element.16.refs_1_, ...), custom_call_target="tpu_custom_call" | custom-call | tf_op jit(solution)/shard_map/pallas_call | solution.py:529

commit v6 on v5

--- a/solution.py
+++ b/solution.py
@@ -212,7 +212,7 @@
         pack(0, order(n))
         return 0
 
-    ahead = 3
+    ahead = 5
     lax.fori_loop(0, ahead, enter_more, 0)
     pl.semaphore_wait(barrier, len(peers))
     def strips_out(rnd, q):
@@ -298,7 +298,7 @@
     middle_chunk(edge_chunk)
     edge_copy(2).start()
 
-    wide = 28
+    wide = 16
     nt = (((1,), (1,)), ((), ()))
 
     def row_block(rows):
@@ -323,7 +323,7 @@
         return carry[0] + one, carry[1] + two
 
     zero = (jnp.zeros((5 * C, 4 * C), F32), jnp.zeros((3 * C, 5 * C), F32))
-    one, two = lax.fori_loop(0, (EXT - HALO) // wide, grads, zero, unroll=2)
+    one, two = lax.fori_loop(0, (EXT - HALO) // wide, grads, zero, unroll=7)
 
     def block(value, i, j):
         return value[C * i : C * (i + 1), C * j : C * (j + 1)]

time: 42.5 us -> 42.9 us (level)
  no operation moved by 1% of the time
where the time goes in v6:
time: 42.9 us; the launch traced here: 42.8 us
  Pallas kernels  42.1 us (98%)
  between operations  0.64 us (1%)
    pallas_call x1, Pallas kernels, shards(): pl.pallas_call(kernel, out_shape=[pltpu.VMEM(field, BF16), pltpu.VMEM(fie...  40.9 us
    pallas_call x1, Pallas kernels, shards(): pl.pallas_call(hand_over, out_shape=[shape(r.shape, r.dtype) for r in res...  1.28 us

profile of v6, /device:TPU:1, one launch (start us, length us, event | category | flops | bytes accessed | tf_op | source)
XLA Modules:
  0.0 42.8 jit_solution(16600137634006364061)
XLA Ops:
  0.6 40.9 %shard_map.110 = (bf16[32,96,128]{2,1,0:T(8,128)(2,1)S(1)}, bf16[32,96,128]{2,1,0:T(8,128)(2,1)S(1)}, f32[9,32,32]{2,1,0:T(8,128)S(1)}, f32[1,32]{1,0:T(1,128)S(1)}, f32[9,32,32]{2,1,0:T(8,128)S(1)}) custom-call(s32[2]{0:T(128)} %rate.1, bf16[32,96,128]{2,1,0:T(8,128)(2,1)} %feat_in.1, bf16[32,96,128]{2,1,0:T(8,128)(2,1)} %cot_in.1, s32[96,128]{1,0:T(8,128)} %mask_in.1, ...), custom_call_target="tpu_custom_call" | custom-call | tf_op jit(solution)/shard_map/pallas_call | solution.py:482
  41.5 1.3 %shard_map.111 = (bf16[32,96,128]{2,1,0:T(8,128)(2,1)}, bf16[32,96,128]{2,1,0:T(8,128)(2,1)}, f32[9,32,32]{2,1,0:T(8,128)}, f32[1,32]{1,0:T(1,128)}, f32[9,32,32]{2,1,0:T(8,128)}) custom-call(bf16[32,96,128]{2,1,0:T(8,128)(2,1)S(1)} %get-tuple-element.15.refs_0_, bf16[32,96,128]{2,1,0:T(8,128)(2,1)S(1)} %get-tuple-element.16.refs_1_, ...), custom_call_target="tpu_custom_call" | custom-call | tf_op jit(solution)/shard_map/pallas_call | solution.py:529
